TPU v7x, 128 devices: a whole 4x4x4 slice. The times are simulated.
128 devices in a mesh: seq: 16 (over x_hi, z, core), ch: 8 (over x_lo, y).
Axes of the slice: x: 4 (x_hi: 2, x_lo: 2; x = x_hi * 2 + x_lo), y: 4, z: 4, core: 2. Of those that a mesh axis runs over, the one named last changes fastest.
Arguments:
- proj_first: bfloat16 [16384, 1024], P('seq', 'ch'), may hold values from -6 to 6
- proj_second: bfloat16 [16384, 1024], P('seq', 'ch'), may hold values from -6 to 6
- out_gate: bfloat16 [16384, 1024], P('seq', 'ch'), may hold values from -6 to 6
- upstream: bfloat16 [16384, 1024], P('seq', 'ch'), may hold values from -6 to 6
- filter_rows: bfloat16 [16384, 1024], P('seq', 'ch'), may hold values from -2 to 2
- conv_first: float32 [3, 1024], P(None, 'ch'), may hold values from -3 to 3
- conv_second: float32 [3, 1024], P(None, 'ch'), may hold values from -3 to 3
- skip_gain: float32 [1024], P('ch'), may hold values from -4 to 4
Outputs:
- grad_first: bfloat16 [16384, 1024], P('seq', 'ch')
- grad_second: bfloat16 [16384, 1024], P('seq', 'ch')
- filter_grad: float32 [16384, 1024], P('seq', 'ch')
All inputs are finite; a program needn't handle non-finite values.
Results may differ from a plain program's by a relative error of at most 0.012.
Values may be sent and summed in bfloat16 or wider, within the bound.
A program may use at most 128 MiB of HBM per device.

v0:
```python
from functools import partial

import jax
import jax.numpy as jnp
from jax import lax
from jax.experimental import pallas as pl
from jax.experimental.pallas import tpu as pltpu
from jax.sharding import PartitionSpec as P

f32 = jnp.float32
bf16 = jnp.bfloat16
MESH = pl.DeviceIdType.MESH
N = 16
LANES = 128
TOK = 1024
EXT = TOK + 16
OWN = 8
BLOCKS = 128
EDGE = 16


def rows_of(block):
    return pl.ds(pl.multiple_of(block, 16), 16)


def kernel(
    pf, ps, og, up, fr, c1, c2, sk,
    out_first, out_second, out_filter,
    halo, sbuf, rbuf, ybuf, rmix, rcor,
    pfx, psx, fc, sc, gg, fg, sg,
    gin, fin, frp, ls, acc, y,
    halo_send, halo_recv, send_sem, recv_sem, local_sem,
):
    me = lax.axis_index("seq")
    nxt = lax.rem(me + 1, N)
    prv = lax.rem(me + N - 1, N)

    barrier = pltpu.get_barrier_semaphore()

    def greet(k, _):
        pl.semaphore_signal(
            barrier, inc=1, device_id={"seq": lax.rem(me + k, N)}, device_id_type=MESH
        )
        return 0

    lax.fori_loop(1, N, greet, 0)

    row = lax.broadcasted_iota(jnp.int32, (LANES, LANES), 0)
    col = lax.broadcasted_iota(jnp.int32, (LANES, LANES), 1)
    eye = (row == col).astype(f32).astype(bf16)
    flip = (row + col == LANES - 1).astype(f32).astype(bf16)

    def turned(block):
        return lax.dot_general(
            eye, block, (((1,), (1,)), ((), ())), preferred_element_type=f32
        )

    def flipped(block):
        back = jnp.dot(flip, block, preferred_element_type=f32).astype(bf16)
        return turned(back)

    def put(slot, pair, one, two):
        both = jnp.concatenate(
            [one.reshape(N, OWN, LANES), two.reshape(N, OWN, LANES)], axis=1
        )
        sbuf[slot, :, 16 * pair : 16 * pair + 16, :] = both.astype(bf16)

    def block(ref, i):
        return ref[LANES * i : LANES * (i + 1), :]

    def exchange(slot):
        def go(k, _):
            to = lax.rem(me + k, N)
            pltpu.make_async_remote_copy(
                src_ref=sbuf.at[slot, to],
                dst_ref=rbuf.at[slot, me],
                send_sem=send_sem.at[slot, to],
                recv_sem=recv_sem.at[slot, me],
                device_id={"seq": to},
                device_id_type=MESH,
            ).start()
            return 0

        lax.fori_loop(1, N, go, 0)
        pltpu.make_async_copy(
            sbuf.at[slot, me], rbuf.at[slot, me], local_sem.at[slot]
        ).start()

    def arrived(slot):
        def go(k, _):
            frm = lax.rem(me + k, N)
            pltpu.make_async_remote_copy(
                src_ref=sbuf.at[slot, frm],
                dst_ref=rbuf.at[slot, frm],
                send_sem=send_sem.at[slot, frm],
                recv_sem=recv_sem.at[slot, frm],
                device_id={"seq": frm},
                device_id_type=MESH,
            ).wait()
            return 0

        pltpu.make_async_copy(
            sbuf.at[slot, me], rbuf.at[slot, me], local_sem.at[slot]
        ).wait()
        lax.fori_loop(1, N, go, 0)

    gg[0:TOK, :] = (og[...].astype(f32) * up[...].astype(f32)).astype(bf16)
    for i in range(4):
        put(0, i, turned(block(gg, 2 * i)), turned(block(gg, 2 * i + 1)))
    pl.semaphore_wait(barrier, N - 1)

    halos = [
        (pf, TOK - EDGE, nxt),
        (ps, TOK - EDGE, nxt),
        (pf, 0, prv),
        (ps, 0, prv),
        (og, 0, prv),
        (up, 0, prv),
    ]
    halo_copies = [
        pltpu.make_async_remote_copy(
            src_ref=ref.at[pl.ds(start, EDGE), :],
            dst_ref=halo.at[n],
            send_sem=halo_send.at[n],
            recv_sem=halo_recv.at[n],
            device_id={"seq": to},
            device_id_type=MESH,
        )
        for n, (ref, start, to) in enumerate(halos)
    ]
    for copy in halo_copies:
        copy.start()
    exchange(0)

    for half in range(2):
        for p in range(2):
            put(
                1,
                2 * half + p,
                flipped(block(fr, 2 * (3 - 2 * p) + half)),
                flipped(block(fr, 2 * (2 - 2 * p) + half)),
            )
    exchange(1)

    for copy in halo_copies:
        copy.wait()
    before = me > 0
    after = me < N - 1
    for x, src, n in ((pfx, pf, 0), (psx, ps, 1)):
        x[0:EDGE, :] = jnp.where(before, halo[n].astype(f32), 0.0)
        x[EDGE : EDGE + TOK, :] = src[...].astype(f32)
        x[EDGE + TOK :, :] = halo[n + 2].astype(f32)
    gg[TOK:, :] = jnp.where(after, halo[4].astype(f32) * halo[5].astype(f32), 0.0).astype(bf16)
    for x, w, dst in ((pfx, c1, fc), (psx, c2, sc)):
        dst[...] = (
            w[0:1, :] * x[EDGE : EDGE + EXT, :]
            + w[1:2, :] * x[EDGE - 1 : EDGE - 1 + EXT, :]
            + w[2:3, :] * x[EDGE - 2 : EDGE - 2 + EXT, :]
        )

    def prod(i):
        return (block(fc, i) * block(sc, i)).astype(bf16)

    for half in range(2):
        for p in range(2):
            put(
                2,
                2 * half + p,
                flipped(prod(2 * (3 - 2 * p) + half)),
                flipped(prod(2 * (2 - 2 * p) + half)),
            )
    exchange(2)

    frp[...] = jnp.zeros_like(frp)
    gin[BLOCKS:, :, :] = jnp.zeros((gin.shape[0] - BLOCKS, OWN, LANES), f32)
    y[0, 64, :, :, :] = jnp.zeros((2, OWN, LANES), f32)

    arrived(0)
    gin[0:BLOCKS, :, :] = rbuf[0].astype(f32).reshape(BLOCKS, OWN, LANES)
    for slot in (1, 2):
        arrived(slot)

        def unpack(s, _, slot=slot):
            rows = rbuf[slot, N - 1 - s].astype(f32).reshape(2, 4, OWN, LANES)
            fin[slot - 1, :, pl.ds(4 * s, 4), :, :] = rows
            return 0

        lax.fori_loop(0, N, unpack, 0)

    mask = col <= row

    def rolled(jj, ch):
        line = gin[jj, pl.ds(ch, 1), :]
        return pltpu.roll(
            jnp.broadcast_to(line, (LANES, LANES)), 1, 1, stride=1, stride_axis=0
        )

    def channel(ch, _):
        for f in range(2):
            for h in range(2):
                frp[f, h, 0:64, :] = fin[f, h, :, ch, :]

        def shift(r, _):
            for f in range(2):
                for h in range(2):
                    ls[r, f, :, h * LANES : (h + 1) * LANES] = frp[
                        f, h, pl.ds(r, 112), :
                    ].astype(bf16)
            return 0

        lax.fori_loop(0, 16, shift, 0)
        r1 = rolled(1, ch)
        h0 = jnp.where(mask, rolled(0, ch), r1).astype(bf16)
        acc[...] = jnp.zeros_like(acc)
        for group in range(4):
            rows = 16 * (group + 1)
            tot = jnp.zeros((2 * rows, 2 * LANES), f32)
            for k in range(16):
                j = 16 * group + k
                r2 = rolled(2 * j + 2, ch)
                r3 = rolled(2 * j + 3, ch)
                h1 = jnp.where(mask, r1, r2).astype(bf16)
                h2 = jnp.where(mask, r2, r3).astype(bf16)
                rhs = jnp.concatenate(
                    [jnp.concatenate([h0, h1], 1), jnp.concatenate([h1, h2], 1)], 0
                )
                top = 16 * (3 - group)
                lhs = ls[15 - k, :, top : top + rows, :].reshape(2 * rows, 2 * LANES)
                tot += jnp.dot(lhs, rhs, preferred_element_type=f32)
                r1, h0 = r3, h2
            acc[:, 0:rows, :] += tot.reshape(2, rows, 2 * LANES)
        for f in range(2):
            for h in range(2):
                y[f, 0:64, h, ch, :] = acc[f, :, h * LANES : (h + 1) * LANES]
        return 0

    lax.fori_loop(0, OWN, channel, 0)

    ybuf[0] = y[0].reshape(65 * 2 * OWN, LANES).astype(bf16)
    ybuf[1, 0:1024, :] = (
        y[1, 0:64].reshape(1024, LANES) * (TOK * N) ** -0.5
    ).astype(bf16)

    def home(f, to, frm):
        dst, size = ((rmix, 80), (rcor, 64))[f]
        return ybuf.at[f, pl.ds(pl.multiple_of(64 * to, 64), size), :], dst.at[frm]

    def back(k, _):
        to = lax.rem(me + k, N)
        for f in range(2):
            src, dst = home(f, to, me)
            pltpu.make_async_remote_copy(
                src_ref=src,
                dst_ref=dst,
                send_sem=send_sem.at[3 + f, to],
                recv_sem=recv_sem.at[3 + f, me],
                device_id={"seq": to},
                device_id_type=MESH,
            ).start()
        return 0

    def back_done(k, _):
        frm = lax.rem(me + k, N)
        for f in range(2):
            src, dst = home(f, frm, frm)
            pltpu.make_async_remote_copy(
                src_ref=src,
                dst_ref=dst,
                send_sem=send_sem.at[3 + f, frm],
                recv_sem=recv_sem.at[3 + f, frm],
                device_id={"seq": frm},
                device_id_type=MESH,
            ).wait()
        return 0

    lax.fori_loop(1, N, back, 0)
    for f in range(2):
        src, dst = home(f, me, me)
        pltpu.make_async_copy(src, dst, local_sem.at[3 + f]).start()
    for f in range(2):
        src, dst = home(f, me, me)
        pltpu.make_async_copy(src, dst, local_sem.at[3 + f]).wait()
    lax.fori_loop(1, N, back_done, 0)

    def columns(ref, pair):
        both = ref[:, 16 * pair : 16 * pair + 16, :].astype(f32)
        both = both.reshape(N, 2, OWN, LANES)
        return [jnp.transpose(both[:, n].reshape(LANES, LANES)) for n in range(2)]

    skip = sk[...]

    def grads(start, size, mix):
        at = pl.ds(start, size)
        total = mix + skip * gg[at, :].astype(f32)
        fg[at, :] = (total * sc[at, :]).astype(bf16).astype(f32)
        sg[at, :] = (total * fc[at, :]).astype(bf16).astype(f32)

    for pair in range(4):
        one, two = columns(rmix, pair)
        grads(256 * pair, LANES, one)
        grads(256 * pair + LANES, LANES, two)
        one, two = columns(rcor, pair)
        out_filter[256 * pair : 256 * pair + LANES, :] = one
        out_filter[256 * pair + LANES : 256 * pair + 256, :] = two
    grads(TOK, EXT - TOK, columns(rmix, 4)[0][0 : EXT - TOK])
    for x, w, dst in ((fg, c1, out_first), (sg, c2, out_second)):
        dst[...] = (
            w[0:1, :] * x[0:TOK, :]
            + w[1:2, :] * x[1 : TOK + 1, :]
            + w[2:3, :] * x[2 : TOK + 2, :]
        ).astype(bf16)


def body(pf, ps, og, up, fr, c1, c2, sk):
    vmem = pl.BlockSpec(memory_space=pltpu.VMEM)
    dma = pltpu.SemaphoreType.DMA
    return pl.pallas_call(
        kernel,
        out_shape=(
            jax.ShapeDtypeStruct((TOK, LANES), bf16),
            jax.ShapeDtypeStruct((TOK, LANES), bf16),
            jax.ShapeDtypeStruct((TOK, LANES), f32),
        ),
        in_specs=[vmem] * 8,
        out_specs=(vmem,) * 3,
        scratch_shapes=[
            pltpu.VMEM((6, EDGE, LANES), bf16),
            pltpu.VMEM((3, N, 64, LANES), bf16),
            pltpu.VMEM((3, N, 64, LANES), bf16),
            pltpu.VMEM((2, 1040, LANES), bf16),
            pltpu.VMEM((N, 80, LANES), bf16),
            pltpu.VMEM((N, 64, LANES), bf16),
            pltpu.VMEM((EDGE + EXT, LANES), f32),
            pltpu.VMEM((EDGE + EXT, LANES), f32),
            pltpu.VMEM((EXT, LANES), f32),
            pltpu.VMEM((EXT, LANES), f32),
            pltpu.VMEM((EXT, LANES), bf16),
            pltpu.VMEM((EXT, LANES), f32),
            pltpu.VMEM((EXT, LANES), f32),
            pltpu.VMEM((BLOCKS + 2, OWN, LANES), f32),
            pltpu.VMEM((2, 2, 64, OWN, LANES), f32),
            pltpu.VMEM((2, 2, 128, LANES), f32),
            pltpu.VMEM((16, 2, 112, 2 * LANES), bf16),
            pltpu.VMEM((2, 64, 2 * LANES), f32),
            pltpu.VMEM((2, 65, 2, OWN, LANES), f32),
            dma((6,)),
            dma((6,)),
            dma((5, N)),
            dma((5, N)),
            dma((5,)),
        ],
        compiler_params=pltpu.CompilerParams(
            collective_id=0, has_side_effects=True, vmem_limit_bytes=48 * 2**20
        ),
        cost_estimate=pl.CostEstimate(
            flops=2 * 4 * 10**9, bytes_accessed=3 * 10**6, transcendentals=0
        ),
    )(pf, ps, og, up, fr, c1, c2, sk.reshape(1, LANES))


def solution(mesh):
    tok = P("seq", "ch")
    return jax.shard_map(
        body,
        mesh=mesh,
        in_specs=(tok,) * 5 + (P(None, "ch"), P(None, "ch"), P("ch")),
        out_specs=(tok,) * 3,
        check_vma=False,
    )
```

profile of v0, /device:TPU:1, one launch (start us, length us, event | category | flops | bytes accessed | tf_op | source)
XLA Modules:
  0.0 59.6 jit_solution(10454193122981476949)
XLA Ops:
  0.6 0.0 copy-start.7
  0.6 0.6 %copy-done.7 = f32[128]{0:T(128)S(1)} copy-done((f32[128]{0:T(128)S(1)}, f32[128]{0:T(128)}, u32[]{:S(2)}) %copy-start.7) | copy-done | bytes 536
  1.3 0.0 copy-start
  1.3 0.9 %copy-done = bf16[1024,128]{1,0:T(8,128)(2,1)S(1)} copy-done((bf16[1024,128]{1,0:T(8,128)(2,1)S(1)}, bf16[1024,128]{1,0:T(8,128)(2,1)}, u32[]{:S(2)}) %copy-start) | copy-done | bytes 262168
  2.2 0.0 copy-start.1
  2.2 0.9 %copy-done.1 = bf16[1024,128]{1,0:T(8,128)(2,1)S(1)} copy-done((bf16[1024,128]{1,0:T(8,128)(2,1)S(1)}, bf16[1024,128]{1,0:T(8,128)(2,1)}, u32[]{:S(2)}) %copy-start.1) | copy-done | bytes 262168
  3.2 0.0 copy-start.2
  3.2 0.9 %copy-done.2 = bf16[1024,128]{1,0:T(8,128)(2,1)S(1)} copy-done((bf16[1024,128]{1,0:T(8,128)(2,1)S(1)}, bf16[1024,128]{1,0:T(8,128)(2,1)}, u32[]{:S(2)}) %copy-start.2) | copy-done | bytes 262168
  4.1 0.0 copy-start.3
  4.1 0.9 %copy-done.3 = bf16[1024,128]{1,0:T(8,128)(2,1)S(1)} copy-done((bf16[1024,128]{1,0:T(8,128)(2,1)S(1)}, bf16[1024,128]{1,0:T(8,128)(2,1)}, u32[]{:S(2)}) %copy-start.3) | copy-done | bytes 262168
  5.1 0.0 copy-start.4
  5.1 0.9 %copy-done.4 = bf16[1024,128]{1,0:T(8,128)(2,1)S(1)} copy-done((bf16[1024,128]{1,0:T(8,128)(2,1)S(1)}, bf16[1024,128]{1,0:T(8,128)(2,1)}, u32[]{:S(2)}) %copy-start.4) | copy-done | bytes 262168
  6.0 0.0 copy-start.5
  6.0 0.7 %copy-done.5 = f32[3,128]{1,0:T(4,128)S(1)} copy-done((f32[3,128]{1,0:T(4,128)S(1)}, f32[3,128]{1,0:T(4,128)}, u32[]{:S(2)}) %copy-start.5) | copy-done | bytes 1560
  6.7 0.0 copy-start.6
  6.7 0.7 %copy-done.6 = f32[3,128]{1,0:T(4,128)S(1)} copy-done((f32[3,128]{1,0:T(4,128)S(1)}, f32[3,128]{1,0:T(4,128)}, u32[]{:S(2)}) %copy-start.6) | copy-done | bytes 1560
  7.4 50.0 %shard_map.103 = (bf16[1024,128]{1,0:T(8,128)(2,1)S(1)}, bf16[1024,128]{1,0:T(8,128)(2,1)S(1)}, f32[1024,128]{1,0:T(8,128)S(1)}) custom-call(bf16[1024,128]{1,0:T(8,128)(2,1)S(1)} %copy-done, bf16[1024,128]{1,0:T(8,128)(2,1)S(1)} %copy-done.1, bf16[1024,128]{1,0:T(8,128)(2,1)S(1)} %copy-done.2, bf16[1024,128]{1,0:T(8,128)(2,1)S(1)} %copy-done.3, ...), custom_call_target="tpu_custom_call" | custom-call | flops 8000000000 | bytes 3000000 | tf_op jit(solution)/shard_map/pallas_call | solution.py:317
  57.4 0.7 %copy.14 = bf16[1024,128]{1,0:T(8,128)(2,1)} copy(bf16[1024,128]{1,0:T(8,128)(2,1)S(1)} %get-tuple-element.6) | data formatting | bytes 524288
  58.1 0.7 %copy.15 = bf16[1024,128]{1,0:T(8,128)(2,1)} copy(bf16[1024,128]{1,0:T(8,128)(2,1)S(1)} %get-tuple-element.7) | data formatting | bytes 524288
  58.8 0.8 %copy.16 = f32[1024,128]{1,0:T(8,128)} copy(f32[1024,128]{1,0:T(8,128)S(1)} %get-tuple-element.8) | data formatting | bytes 1048576
Async XLA Ops:
  0.6 0.7 %copy-start.7 = (f32[128]{0:T(128)S(1)}, f32[128]{0:T(128)}, u32[]{:S(2)}) copy-start(f32[128]{0:T(128)} %param.15) | copy-start | bytes 1540
  1.3 0.9 %copy-start = (bf16[1024,128]{1,0:T(8,128)(2,1)S(1)}, bf16[1024,128]{1,0:T(8,128)(2,1)}, u32[]{:S(2)}) copy-start(bf16[1024,128]{1,0:T(8,128)(2,1)} %pf.1) | copy-start | bytes 786436
  2.2 0.9 %copy-start.1 = (bf16[1024,128]{1,0:T(8,128)(2,1)S(1)}, bf16[1024,128]{1,0:T(8,128)(2,1)}, u32[]{:S(2)}) copy-start(bf16[1024,128]{1,0:T(8,128)(2,1)} %ps.1) | copy-start | bytes 786436
  3.2 0.9 %copy-start.2 = (bf16[1024,128]{1,0:T(8,128)(2,1)S(1)}, bf16[1024,128]{1,0:T(8,128)(2,1)}, u32[]{:S(2)}) copy-start(bf16[1024,128]{1,0:T(8,128)(2,1)} %og.1) | copy-start | bytes 786436
  4.1 0.9 %copy-start.3 = (bf16[1024,128]{1,0:T(8,128)(2,1)S(1)}, bf16[1024,128]{1,0:T(8,128)(2,1)}, u32[]{:S(2)}) copy-start(bf16[1024,128]{1,0:T(8,128)(2,1)} %up.1) | copy-start | bytes 786436
  5.1 0.9 %copy-start.4 = (bf16[1024,128]{1,0:T(8,128)(2,1)S(1)}, bf16[1024,128]{1,0:T(8,128)(2,1)}, u32[]{:S(2)}) copy-start(bf16[1024,128]{1,0:T(8,128)(2,1)} %fr.1) | copy-start | bytes 786436
  6.0 0.7 %copy-start.5 = (f32[3,128]{1,0:T(4,128)S(1)}, f32[3,128]{1,0:T(4,128)}, u32[]{:S(2)}) copy-start(f32[3,128]{1,0:T(4,128)} %c1.1) | copy-start | bytes 4612
  6.7 0.7 %copy-start.6 = (f32[3,128]{1,0:T(4,128)S(1)}, f32[3,128]{1,0:T(4,128)}, u32[]{:S(2)}) copy-start(f32[3,128]{1,0:T(4,128)} %c2.1) | copy-start | bytes 4612
where the time goes:
time: 59.9 us; the launch traced here: 59.6 us
  Pallas kernels  50 us (83%)
  local copies, waits for them, and re-layouts  8.96 us (15%)
  between operations  0.66 us (1%)
    pallas_call x1, Pallas kernels, body(): pl.pallas_call(kernel, out_shape=(jax.ShapeDtypeStruct((TOK, LANES), bf16...  50 us
    unnamed x19, local copies, waits for them, and re-layouts  8.96 us

commit v1 on v0

--- a/solution.py
+++ b/solution.py
@@ -24,12 +24,13 @@
 
 
 def kernel(
+    pf_in, ps_in, og_in, up_in, fr_in, c1_in, c2_in, sk_in,
+    out_first, out_second, out_filter,
     pf, ps, og, up, fr, c1, c2, sk,
-    out_first, out_second, out_filter,
     halo, sbuf, rbuf, ybuf, rmix, rcor,
     pfx, psx, fc, sc, gg, fg, sg,
     gin, fin, frp, ls, acc, y,
-    halo_send, halo_recv, send_sem, recv_sem, local_sem,
+    halo_send, halo_recv, send_sem, recv_sem, local_sem, in_sem,
 ):
     me = lax.axis_index("seq")
     nxt = lax.rem(me + 1, N)
@@ -44,6 +45,24 @@
         return 0
 
     lax.fori_loop(1, N, greet, 0)
+
+    fetched = [
+        pltpu.make_async_copy(src, dst, in_sem.at[n])
+        for n, (src, dst) in enumerate(
+            (
+                (og_in, og),
+                (up_in, up),
+                (fr_in, fr),
+                (pf_in, pf),
+                (ps_in, ps),
+                (c1_in, c1),
+                (c2_in, c2),
+                (sk_in, sk),
+            )
+        )
+    ]
+    for copy in fetched:
+        copy.start()
 
     row = lax.broadcasted_iota(jnp.int32, (LANES, LANES), 0)
     col = lax.broadcasted_iota(jnp.int32, (LANES, LANES), 1)
@@ -104,18 +123,20 @@
         ).wait()
         lax.fori_loop(1, N, go, 0)
 
+    fetched[0].wait()
+    fetched[1].wait()
     gg[0:TOK, :] = (og[...].astype(f32) * up[...].astype(f32)).astype(bf16)
     for i in range(4):
         put(0, i, turned(block(gg, 2 * i)), turned(block(gg, 2 * i + 1)))
     pl.semaphore_wait(barrier, N - 1)
 
     halos = [
-        (pf, TOK - EDGE, nxt),
-        (ps, TOK - EDGE, nxt),
-        (pf, 0, prv),
-        (ps, 0, prv),
-        (og, 0, prv),
-        (up, 0, prv),
+        (pf_in, TOK - EDGE, nxt),
+        (ps_in, TOK - EDGE, nxt),
+        (pf_in, 0, prv),
+        (ps_in, 0, prv),
+        (og_in, 0, prv),
+        (up_in, 0, prv),
     ]
     halo_copies = [
         pltpu.make_async_remote_copy(
@@ -132,6 +153,7 @@
         copy.start()
     exchange(0)
 
+    fetched[2].wait()
     for half in range(2):
         for p in range(2):
             put(
@@ -142,6 +164,8 @@
             )
     exchange(1)
 
+    for copy in fetched[3:]:
+        copy.wait()
     for copy in halo_copies:
         copy.wait()
     before = me > 0
@@ -203,31 +227,32 @@
         def shift(r, _):
             for f in range(2):
                 for h in range(2):
-                    ls[r, f, :, h * LANES : (h + 1) * LANES] = frp[
-                        f, h, pl.ds(r, 112), :
-                    ].astype(bf16)
+                    ls[r, f, h] = frp[f, h, pl.ds(r, 112), :].astype(bf16)
             return 0
 
-        lax.fori_loop(0, 16, shift, 0)
+        lax.fori_loop(0, 16, shift, 0, unroll=True)
         r1 = rolled(1, ch)
         h0 = jnp.where(mask, rolled(0, ch), r1).astype(bf16)
         acc[...] = jnp.zeros_like(acc)
         for group in range(4):
             rows = 16 * (group + 1)
-            tot = jnp.zeros((2 * rows, 2 * LANES), f32)
+            left, right = [], []
             for k in range(16):
                 j = 16 * group + k
                 r2 = rolled(2 * j + 2, ch)
                 r3 = rolled(2 * j + 3, ch)
                 h1 = jnp.where(mask, r1, r2).astype(bf16)
                 h2 = jnp.where(mask, r2, r3).astype(bf16)
-                rhs = jnp.concatenate(
-                    [jnp.concatenate([h0, h1], 1), jnp.concatenate([h1, h2], 1)], 0
-                )
+                right += [jnp.concatenate([h0, h1], 1), jnp.concatenate([h1, h2], 1)]
                 top = 16 * (3 - group)
-                lhs = ls[15 - k, :, top : top + rows, :].reshape(2 * rows, 2 * LANES)
-                tot += jnp.dot(lhs, rhs, preferred_element_type=f32)
+                for h in range(2):
+                    left.append(ls[15 - k, :, h, top : top + rows, :].reshape(2 * rows, LANES))
                 r1, h0 = r3, h2
+            tot = jnp.dot(
+                jnp.concatenate(left, 1),
+                jnp.concatenate(right, 0),
+                preferred_element_type=f32,
+            )
             acc[:, 0:rows, :] += tot.reshape(2, rows, 2 * LANES)
         for f in range(2):
             for h in range(2):
@@ -321,9 +346,12 @@
             jax.ShapeDtypeStruct((TOK, LANES), bf16),
             jax.ShapeDtypeStruct((TOK, LANES), f32),
         ),
-        in_specs=[vmem] * 8,
+        in_specs=[pl.BlockSpec(memory_space=pltpu.HBM)] * 8,
         out_specs=(vmem,) * 3,
         scratch_shapes=[
+            *[pltpu.VMEM((TOK, LANES), bf16)] * 5,
+            *[pltpu.VMEM((3, LANES), f32)] * 2,
+            pltpu.VMEM((1, LANES), f32),
             pltpu.VMEM((6, EDGE, LANES), bf16),
             pltpu.VMEM((3, N, 64, LANES), bf16),
             pltpu.VMEM((3, N, 64, LANES), bf16),
@@ -340,7 +368,7 @@
             pltpu.VMEM((BLOCKS + 2, OWN, LANES), f32),
             pltpu.VMEM((2, 2, 64, OWN, LANES), f32),
             pltpu.VMEM((2, 2, 128, LANES), f32),
-            pltpu.VMEM((16, 2, 112, 2 * LANES), bf16),
+            pltpu.VMEM((16, 2, 2, 112, LANES), bf16),
             pltpu.VMEM((2, 64, 2 * LANES), f32),
             pltpu.VMEM((2, 65, 2, OWN, LANES), f32),
             dma((6,)),
@@ -348,9 +376,10 @@
             dma((5, N)),
             dma((5, N)),
             dma((5,)),
+            dma((8,)),
         ],
         compiler_params=pltpu.CompilerParams(
-            collective_id=0, has_side_effects=True, vmem_limit_bytes=48 * 2**20
+            collective_id=0, has_side_effects=True, vmem_limit_bytes=56 * 2**20
         ),
         cost_estimate=pl.CostEstimate(
             flops=2 * 4 * 10**9, bytes_accessed=3 * 10**6, transcendentals=0

time: 59.9 us -> 52 us (0.87)
  local copies, waits for them, and re-layouts: 8.96 us -> 3.24 us
  Pallas kernels: 50 us -> 47.9 us
    unnamed x19 -> x7, local copies, waits for them, and re-layouts: 8.96 us -> 3.24 us
    pallas_call x1, Pallas kernels: 50 us -> 47.9 us  [body(): pl.pallas_call(kernel, out_shape=(jax.ShapeDtypeStruct((TOK, LANES), bf16...]
where the time goes in v1:
time: 52 us; the launch traced here: 51.8 us
  Pallas kernels  47.9 us (92%)
  local copies, waits for them, and re-layouts  3.24 us (6%)
  between operations  0.66 us (1%)
    pallas_call x1, Pallas kernels, body(): pl.pallas_call(kernel, out_shape=(jax.ShapeDtypeStruct((TOK, LANES), bf16...  47.9 us
    unnamed x7, local copies, waits for them, and re-layouts  3.24 us

profile of v1, /device:TPU:1, one launch (start us, length us, event | category | flops | bytes accessed | tf_op | source)
XLA Modules:
  0.0 51.8 jit_solution(14059474108491197643)
XLA Ops:
  0.6 47.9 %shard_map.103 = (bf16[1024,128]{1,0:T(8,128)(2,1)}, bf16[1024,128]{1,0:T(8,128)(2,1)}, f32[1024,128]{1,0:T(8,128)}) custom-call(bf16[1024,128]{1,0:T(8,128)(2,1)} %pf_in.1, bf16[1024,128]{1,0:T(8,128)(2,1)} %ps_in.1, bf16[1024,128]{1,0:T(8,128)(2,1)} %og_in.1, bf16[1024,128]{1,0:T(8,128)(2,1)} %up_in.1, bf16[1024,128]{1,0:T(8,128)(2,1)} %fr_in.1, ...), custom_call_target="tpu_custom_call" | custom-call | flops 8000000000 | bytes 3000000 | tf_op jit(solution)/shard_map/pallas_call | solution.py:342
  48.5 0.0 copy-start.1
  48.6 0.0 copy-start
  48.6 1.7 %copy.14 = bf16[1024,128]{1,0:T(8,128)(2,1)} copy(bf16[1024,128]{1,0:T(8,128)(2,1)} %get-tuple-element.6) | data formatting | bytes 524288
  50.3 0.0 copy-done.1
  50.3 0.7 %copy.15 = bf16[1024,128]{1,0:T(8,128)(2,1)} copy(bf16[1024,128]{1,0:T(8,128)(2,1)S(1)} %copy-done.1) | data formatting | bytes 524288
  51.0 0.0 copy-done
  51.0 0.8 %copy.16 = f32[1024,128]{1,0:T(8,128)} copy(f32[1024,128]{1,0:T(8,128)S(1)} %copy-done) | data formatting | bytes 1048576
Async XLA Ops:
  48.5 1.8 %copy-start.1 = (bf16[1024,128]{1,0:T(8,128)(2,1)S(1)}, bf16[1024,128]{1,0:T(8,128)(2,1)}, u32[]{:S(2)}) copy-start(bf16[1024,128]{1,0:T(8,128)(2,1)} %get-tuple-element.7) | copy-start | bytes 786436
  48.6 2.5 %copy-start = (f32[1024,128]{1,0:T(8,128)S(1)}, f32[1024,128]{1,0:T(8,128)}, u32[]{:S(2)}) copy-start(f32[1024,128]{1,0:T(8,128)} %get-tuple-element.8) | copy-start | bytes 1572868

commit v2 on v1

v2 whole, which is shorter than its diff:
```python
from functools import partial

import jax
import jax.numpy as jnp
from jax import lax
from jax.experimental import pallas as pl
from jax.experimental.pallas import tpu as pltpu
from jax.sharding import PartitionSpec as P

f32 = jnp.float32
bf16 = jnp.bfloat16
MESH = pl.DeviceIdType.MESH
N = 16
LANES = 128
TOK = 1024
EXT = TOK + 16
OWN = 8
EDGE = 16


def kernel(
    pf_in, ps_in, og_in, up_in, fr_in, c1_in, c2_in, sk_in,
    out_first, out_second, out_filter,
    pf, ps, og, up, fr, c1, c2, sk,
    halo, sbuf, rbuf, ybuf, rret, tok,
    pfx, psx, fc, sc, gg, fg, sg,
    gin, fin, frp, ls, acc, y,
    halo_send, halo_recv, send_sem, recv_sem, local_sem, in_sem,
):
    me = lax.axis_index("seq")
    nxt = lax.rem(me + 1, N)
    prv = lax.rem(me + N - 1, N)

    barrier = pltpu.get_barrier_semaphore()

    def greet(k, _):
        pl.semaphore_signal(
            barrier, inc=1, device_id={"seq": lax.rem(me + k, N)}, device_id_type=MESH
        )
        return 0

    lax.fori_loop(1, N, greet, 0)

    fetched = [
        pltpu.make_async_copy(src, dst, in_sem.at[n])
        for n, (src, dst) in enumerate(
            (
                (og_in, og),
                (up_in, up),
                (fr_in, fr),
                (pf_in, pf),
                (ps_in, ps),
                (c1_in, c1),
                (c2_in, c2),
                (sk_in, sk),
            )
        )
    ]
    for copy in fetched:
        copy.start()

    row = lax.broadcasted_iota(jnp.int32, (LANES, LANES), 0)
    col = lax.broadcasted_iota(jnp.int32, (LANES, LANES), 1)
    flip = (row + col == LANES - 1).astype(f32).astype(bf16)
    row2 = lax.broadcasted_iota(jnp.int32, (256, 256), 0)
    col2 = lax.broadcasted_iota(jnp.int32, (256, 256), 1)
    picked = ((row2 & 4) << 5) + (row2 & 120) + ((row2 >> 7) << 2) + (row2 & 3)
    pick = (picked == col2).astype(f32).astype(bf16)

    def put(base, blocks):
        pairs = [jnp.concatenate(blocks[2 * q : 2 * q + 2], axis=1) for q in range(4)]
        turned = lax.dot_general(
            pick,
            jnp.concatenate(pairs, axis=0),
            (((1,), (1,)), ((), ())),
            preferred_element_type=f32,
        )
        for n in range(2):
            both = jnp.concatenate(
                [
                    turned[:, LANES * q : LANES * (q + 1)].reshape(2, N, OWN, LANES)
                    for q in (2 * n, 2 * n + 1)
                ],
                axis=2,
            ).astype(bf16)
            for half in range(2):
                sbuf[half, :, base + 16 * n : base + 16 * n + 16, :] = both[half]

    def backwards(blocks):
        wide = jnp.concatenate([blocks[6 - (n & 6) + (n & 1)] for n in range(8)], axis=1)
        back = jnp.dot(flip, wide, preferred_element_type=f32).astype(bf16)
        return [back[:, LANES * n : LANES * (n + 1)] for n in range(8)]

    def blocks_of(ref):
        return [ref[LANES * i : LANES * (i + 1), :] for i in range(8)]

    messages = ((0, 0, 64), (0, 64, 32), (1, 0, 96))

    def exchange(m):
        half, start, size = messages[m]
        part = pl.ds(start, size)

        def go(k, _):
            to = lax.rem(me + k, N)
            pltpu.make_async_remote_copy(
                src_ref=sbuf.at[half, to, part],
                dst_ref=rbuf.at[half, me, part],
                send_sem=send_sem.at[m, to],
                recv_sem=recv_sem.at[m, me],
                device_id={"seq": to},
                device_id_type=MESH,
            ).start()
            return 0

        lax.fori_loop(1, N, go, 0)
        pltpu.make_async_copy(
            sbuf.at[half, me, part], rbuf.at[half, me, part], local_sem.at[m]
        ).start()

    def arrived(m):
        half, start, size = messages[m]
        part = pl.ds(start, size)

        def go(k, _):
            frm = lax.rem(me + k, N)
            pltpu.make_async_remote_copy(
                src_ref=sbuf.at[half, frm, part],
                dst_ref=rbuf.at[half, frm, part],
                send_sem=send_sem.at[m, frm],
                recv_sem=recv_sem.at[m, frm],
                device_id={"seq": frm},
                device_id_type=MESH,
            ).wait()
            return 0

        pltpu.make_async_copy(
            sbuf.at[half, me, part], rbuf.at[half, me, part], local_sem.at[m]
        ).wait()
        lax.fori_loop(1, N, go, 0)

    fetched[0].wait()
    fetched[1].wait()
    gg[0:TOK, :] = (og[...].astype(f32) * up[...].astype(f32)).astype(bf16)
    put(0, blocks_of(gg))
    fetched[2].wait()
    put(32, backwards(blocks_of(fr)))
    pl.semaphore_wait(barrier, N - 1)

    halos = [
        (pf_in, TOK - EDGE, nxt),
        (ps_in, TOK - EDGE, nxt),
        (pf_in, 0, prv),
        (ps_in, 0, prv),
        (og_in, 0, prv),
        (up_in, 0, prv),
    ]
    halo_copies = [
        pltpu.make_async_remote_copy(
            src_ref=ref.at[pl.ds(start, EDGE), :],
            dst_ref=halo.at[n],
            send_sem=halo_send.at[n],
            recv_sem=halo_recv.at[n],
            device_id={"seq": to},
            device_id_type=MESH,
        )
        for n, (ref, start, to) in enumerate(halos)
    ]
    for copy in halo_copies:
        copy.start()
    exchange(0)

    for copy in fetched[3:]:
        copy.wait()
    for copy in halo_copies:
        copy.wait()
    before = me > 0
    after = me < N - 1
    for x, src, n in ((pfx, pf, 0), (psx, ps, 1)):
        x[0:EDGE, :] = jnp.where(before, halo[n].astype(f32), 0.0)
        x[EDGE : EDGE + TOK, :] = src[...].astype(f32)
        x[EDGE + TOK :, :] = halo[n + 2].astype(f32)
    gg[TOK:, :] = jnp.where(after, halo[4].astype(f32) * halo[5].astype(f32), 0.0).astype(bf16)
    for x, w, dst in ((pfx, c1, fc), (psx, c2, sc)):
        dst[...] = (
            w[0:1, :] * x[EDGE : EDGE + EXT, :]
            + w[1:2, :] * x[EDGE - 1 : EDGE - 1 + EXT, :]
            + w[2:3, :] * x[EDGE - 2 : EDGE - 2 + EXT, :]
        )

    put(64, backwards([(f * g).astype(bf16) for f, g in zip(blocks_of(fc), blocks_of(sc))]))
    exchange(1)
    exchange(2)

    frp[...] = jnp.zeros_like(frp)
    gin[64:, :, :] = jnp.zeros((2, OWN, LANES), f32)
    y[64, :, :, :] = jnp.zeros((2, OWN, LANES), f32)

    def unpack_gated(half):
        rows = rbuf[half, :, 0:32, :].astype(f32)
        gin[0:64, :, :] = rows.reshape(64, OWN, LANES)

    def unpack_filter(half, f):
        for s in range(N):
            rows = rbuf[half, N - 1 - s, 32 * f + 32 : 32 * f + 64, :].astype(f32)
            fin[f, 4 * s : 4 * s + 4, :, :] = rows.reshape(4, OWN, LANES)

    mask = col <= row

    def rolled(jj, ch):
        line = gin[jj // 2, pl.ds(4 * (jj % 2) + ch, 1), :]
        return pltpu.roll(
            jnp.broadcast_to(line, (LANES, LANES)), 1, 1, stride=1, stride_axis=0
        )

    def channel(ch, _):
        for f in range(2):
            for h in range(2):
                frp[f, h, 0:64, :] = fin[f, :, 4 * h + ch, :]

        def shift(r, _):
            for f in range(2):
                for h in range(2):
                    ls[r, f, h] = frp[f, h, pl.ds(r, 112), :].astype(bf16)
            return 0

        lax.fori_loop(0, 16, shift, 0, unroll=True)
        r1 = rolled(1, ch)
        h0 = jnp.where(mask, rolled(0, ch), r1).astype(bf16)
        acc[...] = jnp.zeros_like(acc)
        for group in range(4):
            rows = 16 * (group + 1)
            left, right = [], []
            for k in range(16):
                j = 16 * group + k
                r2 = rolled(2 * j + 2, ch)
                r3 = rolled(2 * j + 3, ch)
                h1 = jnp.where(mask, r1, r2).astype(bf16)
                h2 = jnp.where(mask, r2, r3).astype(bf16)
                right += [jnp.concatenate([h0, h1], 1), jnp.concatenate([h1, h2], 1)]
                top = 16 * (3 - group)
                for h in range(2):
                    left.append(ls[15 - k, :, h, top : top + rows, :].reshape(2 * rows, LANES))
                r1, h0 = r3, h2
            tot = jnp.dot(
                jnp.concatenate(left, 1),
                jnp.concatenate(right, 0),
                preferred_element_type=f32,
            )
            acc[:, 0:rows, :] += tot.reshape(2, rows, 2 * LANES)
        for f in range(2):
            for h in range(2):
                y[0:64, h, 4 * f + ch, :] = (
                    acc[f, :, h * LANES : (h + 1) * LANES] * (1.0, (TOK * N) ** -0.5)[f]
                )
        return 0

    def home(half, to, frm):
        rows = pl.ds(pl.multiple_of(64 * to, 64), 80)
        return ybuf.at[half, rows, :], rret.at[half, frm]

    def back(half):
        def go(k, _):
            to = lax.rem(me + k, N)
            src, dst = home(half, to, me)
            pltpu.make_async_remote_copy(
                src_ref=src,
                dst_ref=dst,
                send_sem=send_sem.at[3 + half, to],
                recv_sem=recv_sem.at[3 + half, me],
                device_id={"seq": to},
                device_id_type=MESH,
            ).start()
            return 0

        ybuf[half] = y[...].reshape(65 * 2 * OWN, LANES).astype(bf16)
        lax.fori_loop(1, N, go, 0)
        src, dst = home(half, me, me)
        pltpu.make_async_copy(src, dst, local_sem.at[3 + half]).start()

    def back_done(half):
        def go(k, _):
            frm = lax.rem(me + k, N)
            src, dst = home(half, frm, frm)
            pltpu.make_async_remote_copy(
                src_ref=src,
                dst_ref=dst,
                send_sem=send_sem.at[3 + half, frm],
                recv_sem=recv_sem.at[3 + half, frm],
                device_id={"seq": frm},
                device_id_type=MESH,
            ).wait()
            return 0

        src, dst = home(half, me, me)
        pltpu.make_async_copy(src, dst, local_sem.at[3 + half]).wait()
        lax.fori_loop(1, N, go, 0)

    arrived(0)
    unpack_gated(0)
    unpack_filter(0, 0)
    arrived(1)
    unpack_filter(0, 1)
    lax.fori_loop(0, 4, channel, 0)
    back(0)
    arrived(2)
    unpack_gated(1)
    unpack_filter(1, 0)
    unpack_filter(1, 1)
    lax.fori_loop(0, 4, channel, 0)
    back(1)

    def columns(half, pair):
        both = rret[half, :, 16 * pair : 16 * pair + 16, :].astype(f32)
        both = both.reshape(N, 2, OWN, LANES)
        for n in range(2):
            turned = jnp.transpose(both[:, n].reshape(LANES, LANES))
            at = LANES * (2 * pair + n)
            tok[half, at : at + LANES, :] = turned.astype(bf16)

    skip = sk[...]

    def grads(start, size, mix):
        at = pl.ds(start, size)
        total = mix + skip * gg[at, :].astype(f32)
        fg[at, :] = (total * sc[at, :]).astype(bf16).astype(f32)
        sg[at, :] = (total * fc[at, :]).astype(bf16).astype(f32)

    for half in range(2):
        back_done(half)
        for pair in range(5):
            columns(half, pair)
    for i in range(9):
        size = LANES if i < 8 else EXT - TOK
        at = pl.ds(LANES * i, size)
        both = jnp.dot(
            jnp.concatenate([tok[0, at, :], tok[1, at, :]], axis=1),
            pick,
            preferred_element_type=f32,
        )
        grads(LANES * i, size, both[:, 0:LANES])
        if i < 8:
            out_filter[at, :] = both[:, LANES:]
    for x, w, dst in ((fg, c1, out_first), (sg, c2, out_second)):
        dst[...] = (
            w[0:1, :] * x[0:TOK, :]
            + w[1:2, :] * x[1 : TOK + 1, :]
            + w[2:3, :] * x[2 : TOK + 2, :]
        ).astype(bf16)


def body(pf, ps, og, up, fr, c1, c2, sk):
    vmem = pl.BlockSpec(memory_space=pltpu.VMEM)
    dma = pltpu.SemaphoreType.DMA
    return pl.pallas_call(
        kernel,
        out_shape=(
            jax.ShapeDtypeStruct((TOK, LANES), bf16),
            jax.ShapeDtypeStruct((TOK, LANES), bf16),
            jax.ShapeDtypeStruct((TOK, LANES), f32),
        ),
        in_specs=[pl.BlockSpec(memory_space=pltpu.HBM)] * 8,
        out_specs=(vmem,) * 3,
        scratch_shapes=[
            *[pltpu.VMEM((TOK, LANES), bf16)] * 5,
            *[pltpu.VMEM((3, LANES), f32)] * 2,
            pltpu.VMEM((1, LANES), f32),
            pltpu.VMEM((6, EDGE, LANES), bf16),
            pltpu.VMEM((2, N, 96, LANES), bf16),
            pltpu.VMEM((2, N, 96, LANES), bf16),
            pltpu.VMEM((2, 1040, LANES), bf16),
            pltpu.VMEM((2, N, 80, LANES), bf16),
            pltpu.VMEM((2, 10 * LANES, LANES), bf16),
            pltpu.VMEM((EDGE + EXT, LANES), f32),
            pltpu.VMEM((EDGE + EXT, LANES), f32),
            pltpu.VMEM((EXT, LANES), f32),
            pltpu.VMEM((EXT, LANES), f32),
            pltpu.VMEM((EXT, LANES), bf16),
            pltpu.VMEM((EXT, LANES), f32),
            pltpu.VMEM((EXT, LANES), f32),
            pltpu.VMEM((66, OWN, LANES), f32),
            pltpu.VMEM((2, 64, OWN, LANES), f32),
            pltpu.VMEM((2, 2, 128, LANES), f32),
            pltpu.VMEM((16, 2, 2, 112, LANES), bf16),
            pltpu.VMEM((2, 64, 2 * LANES), f32),
            pltpu.VMEM((65, 2, OWN, LANES), f32),
            dma((6,)),
            dma((6,)),
            dma((5, N)),
            dma((5, N)),
            dma((5,)),
            dma((8,)),
        ],
        compiler_params=pltpu.CompilerParams(
            collective_id=0, has_side_effects=True, vmem_limit_bytes=56 * 2**20
        ),
        cost_estimate=pl.CostEstimate(
            flops=2 * 4 * 10**9, bytes_accessed=3 * 10**6, transcendentals=0
        ),
    )(pf, ps, og, up, fr, c1, c2, sk.reshape(1, LANES))


def solution(mesh):
    tok = P("seq", "ch")
    return jax.shard_map(
        body,
        mesh=mesh,
        in_specs=(tok,) * 5 + (P(None, "ch"), P(None, "ch"), P("ch")),
        out_specs=(tok,) * 3,
        check_vma=False,
    )
```

time: 52 us -> 48 us (0.923)
  Pallas kernels: 47.9 us -> 43.9 us
    pallas_call x1, Pallas kernels: 47.9 us -> 43.9 us  [body(): pl.pallas_call(kernel, out_shape=(jax.ShapeDtypeStruct((TOK, LANES), bf16...]
where the time goes in v2:
time: 48 us; the launch traced here: 47.8 us
  Pallas kernels  43.9 us (91%)
  local copies, waits for them, and re-layouts  3.24 us (7%)
  between operations  0.66 us (1%)
    pallas_call x1, Pallas kernels, body(): pl.pallas_call(kernel, out_shape=(jax.ShapeDtypeStruct((TOK, LANES), bf16...  43.9 us
    unnamed x7, local copies, waits for them, and re-layouts  3.24 us

profile of v2, /device:TPU:1, one launch (start us, length us, event | category | flops | bytes accessed | tf_op | source)
XLA Modules:
  0.0 47.8 jit_solution(13198027380582064072)
XLA Ops:
  0.6 43.9 %shard_map.103 = (bf16[1024,128]{1,0:T(8,128)(2,1)}, bf16[1024,128]{1,0:T(8,128)(2,1)}, f32[1024,128]{1,0:T(8,128)}) custom-call(bf16[1024,128]{1,0:T(8,128)(2,1)} %pf_in.1, bf16[1024,128]{1,0:T(8,128)(2,1)} %ps_in.1, bf16[1024,128]{1,0:T(8,128)(2,1)} %og_in.1, bf16[1024,128]{1,0:T(8,128)(2,1)} %up_in.1, bf16[1024,128]{1,0:T(8,128)(2,1)} %fr_in.1, ...), custom_call_target="tpu_custom_call" | custom-call | flops 8000000000 | bytes 3000000 | tf_op jit(solution)/shard_map/pallas_call | solution.py:354
  44.6 0.0 copy-start.1
  44.6 0.0 copy-start
  44.6 1.7 %copy.14 = bf16[1024,128]{1,0:T(8,128)(2,1)} copy(bf16[1024,128]{1,0:T(8,128)(2,1)} %get-tuple-element.6) | data formatting | bytes 524288
  46.3 0.0 copy-done.1
  46.3 0.7 %copy.15 = bf16[1024,128]{1,0:T(8,128)(2,1)} copy(bf16[1024,128]{1,0:T(8,128)(2,1)S(1)} %copy-done.1) | data formatting | bytes 524288
  47.0 0.0 copy-done
  47.0 0.8 %copy.16 = f32[1024,128]{1,0:T(8,128)} copy(f32[1024,128]{1,0:T(8,128)S(1)} %copy-done) | data formatting | bytes 1048576
Async XLA Ops:
  44.6 1.8 %copy-start.1 = (bf16[1024,128]{1,0:T(8,128)(2,1)S(1)}, bf16[1024,128]{1,0:T(8,128)(2,1)}, u32[]{:S(2)}) copy-start(bf16[1024,128]{1,0:T(8,128)(2,1)} %get-tuple-element.7) | copy-start | bytes 786436
  44.6 2.5 %copy-start = (f32[1024,128]{1,0:T(8,128)S(1)}, f32[1024,128]{1,0:T(8,128)}, u32[]{:S(2)}) copy-start(f32[1024,128]{1,0:T(8,128)} %get-tuple-element.8) | copy-start | bytes 1572868

commit v3 on v2

--- a/solution.py
+++ b/solution.py
@@ -59,13 +59,12 @@
     for copy in fetched:
         copy.start()
 
-    row = lax.broadcasted_iota(jnp.int32, (LANES, LANES), 0)
-    col = lax.broadcasted_iota(jnp.int32, (LANES, LANES), 1)
-    flip = (row + col == LANES - 1).astype(f32).astype(bf16)
     row2 = lax.broadcasted_iota(jnp.int32, (256, 256), 0)
     col2 = lax.broadcasted_iota(jnp.int32, (256, 256), 1)
     picked = ((row2 & 4) << 5) + (row2 & 120) + ((row2 >> 7) << 2) + (row2 & 3)
     pick = (picked == col2).astype(f32).astype(bf16)
+    source = ((row2 & 64) << 1) + ((row2 >> 7) << 6) + 63 - (row2 & 63)
+    flip = (source == col2).astype(f32).astype(bf16)
 
     def put(base, blocks):
         pairs = [jnp.concatenate(blocks[2 * q : 2 * q + 2], axis=1) for q in range(4)]
@@ -86,13 +85,17 @@
             for half in range(2):
                 sbuf[half, :, base + 16 * n : base + 16 * n + 16, :] = both[half]
 
-    def backwards(blocks):
-        wide = jnp.concatenate([blocks[6 - (n & 6) + (n & 1)] for n in range(8)], axis=1)
+    def backwards(quarters):
+        wide = jnp.concatenate(quarters[::-1], axis=1)
         back = jnp.dot(flip, wide, preferred_element_type=f32).astype(bf16)
-        return [back[:, LANES * n : LANES * (n + 1)] for n in range(8)]
-
-    def blocks_of(ref):
-        return [ref[LANES * i : LANES * (i + 1), :] for i in range(8)]
+        return [
+            back[LANES * z : LANES * (z + 1), LANES * q : LANES * (q + 1)]
+            for q in range(4)
+            for z in range(2)
+        ]
+
+    def blocks_of(ref, size):
+        return [ref[size * i : size * (i + 1), :] for i in range(TOK // size)]
 
     messages = ((0, 0, 64), (0, 64, 32), (1, 0, 96))
 
@@ -138,12 +141,6 @@
         ).wait()
         lax.fori_loop(1, N, go, 0)
 
-    fetched[0].wait()
-    fetched[1].wait()
-    gg[0:TOK, :] = (og[...].astype(f32) * up[...].astype(f32)).astype(bf16)
-    put(0, blocks_of(gg))
-    fetched[2].wait()
-    put(32, backwards(blocks_of(fr)))
     pl.semaphore_wait(barrier, N - 1)
 
     halos = [
@@ -167,6 +164,13 @@
     ]
     for copy in halo_copies:
         copy.start()
+
+    fetched[0].wait()
+    fetched[1].wait()
+    gg[0:TOK, :] = (og[...].astype(f32) * up[...].astype(f32)).astype(bf16)
+    put(0, blocks_of(gg, LANES))
+    fetched[2].wait()
+    put(32, backwards(blocks_of(fr, 256)))
     exchange(0)
 
     for copy in fetched[3:]:
@@ -187,9 +191,9 @@
             + w[2:3, :] * x[EDGE - 2 : EDGE - 2 + EXT, :]
         )
 
-    put(64, backwards([(f * g).astype(bf16) for f, g in zip(blocks_of(fc), blocks_of(sc))]))
+    short = zip(blocks_of(fc, 256), blocks_of(sc, 256))
+    put(64, backwards([(f * g).astype(bf16) for f, g in short]))
     exchange(1)
-    exchange(2)
 
     frp[...] = jnp.zeros_like(frp)
     gin[64:, :, :] = jnp.zeros((2, OWN, LANES), f32)
@@ -204,54 +208,60 @@
             rows = rbuf[half, N - 1 - s, 32 * f + 32 : 32 * f + 64, :].astype(f32)
             fin[f, 4 * s : 4 * s + 4, :, :] = rows.reshape(4, OWN, LANES)
 
-    mask = col <= row
+    row = lax.broadcasted_iota(jnp.int32, (64, LANES), 0)
+    col = lax.broadcasted_iota(jnp.int32, (64, LANES), 1)
+    mask = col - row <= 64
+    low = col < 64
 
     def rolled(jj, ch):
         line = gin[jj // 2, pl.ds(4 * (jj % 2) + ch, 1), :]
         return pltpu.roll(
-            jnp.broadcast_to(line, (LANES, LANES)), 1, 1, stride=1, stride_axis=0
+            jnp.broadcast_to(line, (64, LANES)), 65, 1, stride=1, stride_axis=0
         )
 
     def channel(ch, _):
-        for f in range(2):
-            for h in range(2):
-                frp[f, h, 0:64, :] = fin[f, :, 4 * h + ch, :]
-
-        def shift(r, _):
+        for z in range(2):
             for f in range(2):
-                for h in range(2):
-                    ls[r, f, h] = frp[f, h, pl.ds(r, 112), :].astype(bf16)
-            return 0
-
-        lax.fori_loop(0, 16, shift, 0, unroll=True)
-        r1 = rolled(1, ch)
-        h0 = jnp.where(mask, rolled(0, ch), r1).astype(bf16)
+                frp[z, f, 0:64, :] = fin[f, :, 4 * z + ch, :]
+        for r in range(16):
+            for z in range(2):
+                for f in range(2):
+                    ls[r, z, f] = frp[z, f, pl.ds(r, 112), :].astype(bf16)
         acc[...] = jnp.zeros_like(acc)
+        lines = [rolled(0, ch)]
+        hankel = []
+
+        def more_blocks(count):
+            while len(hankel) < count:
+                lines.append(rolled(min(len(lines), 128), ch))
+                hankel.append(jnp.where(mask, lines[-2], lines[-1]).astype(bf16))
+
         for group in range(4):
             rows = 16 * (group + 1)
+            top = 16 * (3 - group)
             left, right = [], []
             for k in range(16):
                 j = 16 * group + k
-                r2 = rolled(2 * j + 2, ch)
-                r3 = rolled(2 * j + 3, ch)
-                h1 = jnp.where(mask, r1, r2).astype(bf16)
-                h2 = jnp.where(mask, r2, r3).astype(bf16)
-                right += [jnp.concatenate([h0, h1], 1), jnp.concatenate([h1, h2], 1)]
-                top = 16 * (3 - group)
-                for h in range(2):
-                    left.append(ls[15 - k, :, h, top : top + rows, :].reshape(2 * rows, LANES))
-                r1, h0 = r3, h2
-            tot = jnp.dot(
-                jnp.concatenate(left, 1),
-                jnp.concatenate(right, 0),
-                preferred_element_type=f32,
-            )
-            acc[:, 0:rows, :] += tot.reshape(2, rows, 2 * LANES)
+                left.append(ls[15 - k, :, :, top : top + rows, :].reshape(4 * rows, LANES))
+                more_blocks(2 * j + 4)
+                for n in (2 * j, 2 * j + 1):
+                    right.append(jnp.concatenate(hankel[n : n + 3], axis=1))
+            left = jnp.concatenate(left, axis=1)
+            right = jnp.concatenate(right, axis=0)
+            both = jnp.dot(left, right[:, 0:256], preferred_element_type=f32)
+            more = jnp.dot(left[2 * rows :], right[:, 256:], preferred_element_type=f32)
+            acc[:, :, 0:rows, 0:256] += both.reshape(2, 2, rows, 256)
+            acc[1, :, 0:rows, 256:] += more.reshape(2, rows, LANES)
         for f in range(2):
+            moved = [
+                pltpu.roll(acc[1, f, :, LANES * n : LANES * (n + 1)], 64, 1)
+                for n in range(3)
+            ]
             for h in range(2):
-                y[0:64, h, 4 * f + ch, :] = (
-                    acc[f, :, h * LANES : (h + 1) * LANES] * (1.0, (TOK * N) ** -0.5)[f]
+                total = acc[0, f, :, LANES * h : LANES * (h + 1)] + jnp.where(
+                    low, moved[h], moved[h + 1]
                 )
+                y[0:64, h, 4 * f + ch, :] = total * (1.0, (TOK * N) ** -0.5)[f]
         return 0
 
     def home(half, to, frm):
@@ -299,6 +309,7 @@
     unpack_gated(0)
     unpack_filter(0, 0)
     arrived(1)
+    exchange(2)
     unpack_filter(0, 1)
     lax.fori_loop(0, 4, channel, 0)
     back(0)
@@ -381,7 +392,7 @@
             pltpu.VMEM((2, 64, OWN, LANES), f32),
             pltpu.VMEM((2, 2, 128, LANES), f32),
             pltpu.VMEM((16, 2, 2, 112, LANES), bf16),
-            pltpu.VMEM((2, 64, 2 * LANES), f32),
+            pltpu.VMEM((2, 2, 64, 3 * LANES), f32),
             pltpu.VMEM((65, 2, OWN, LANES), f32),
             dma((6,)),
             dma((6,)),

time: 48 us -> 44.3 us (0.923)
  Pallas kernels: 43.9 us -> 40.3 us
    pallas_call x1, Pallas kernels: 43.9 us -> 40.3 us  [body(): pl.pallas_call(kernel, out_shape=(jax.ShapeDtypeStruct((TOK, LANES), bf16...]
where the time goes in v3:
time: 44.3 us; the launch traced here: 44.2 us
  Pallas kernels  40.3 us (91%)
  local copies, waits for them, and re-layouts  3.24 us (7%)
  between operations  0.66 us (1%)
    pallas_call x1, Pallas kernels, body(): pl.pallas_call(kernel, out_shape=(jax.ShapeDtypeStruct((TOK, LANES), bf16...  40.3 us
    unnamed x7, local copies, waits for them, and re-layouts  3.24 us

profile of v3, /device:TPU:1, one launch (start us, length us, event | category | flops | bytes accessed | tf_op | source)
XLA Modules:
  0.0 44.2 jit_solution(8628599951604972211)
XLA Ops:
  0.6 40.3 %shard_map.103 = (bf16[1024,128]{1,0:T(8,128)(2,1)}, bf16[1024,128]{1,0:T(8,128)(2,1)}, f32[1024,128]{1,0:T(8,128)}) custom-call(bf16[1024,128]{1,0:T(8,128)(2,1)} %pf_in.1, bf16[1024,128]{1,0:T(8,128)(2,1)} %ps_in.1, bf16[1024,128]{1,0:T(8,128)(2,1)} %og_in.1, bf16[1024,128]{1,0:T(8,128)(2,1)} %up_in.1, bf16[1024,128]{1,0:T(8,128)(2,1)} %fr_in.1, ...), custom_call_target="tpu_custom_call" | custom-call | flops 8000000000 | bytes 3000000 | tf_op jit(solution)/shard_map/pallas_call | solution.py:365
  40.9 0.0 copy-start.1
  40.9 0.0 copy-start
  40.9 1.7 %copy.14 = bf16[1024,128]{1,0:T(8,128)(2,1)} copy(bf16[1024,128]{1,0:T(8,128)(2,1)} %get-tuple-element.6) | data formatting | bytes 524288
  42.7 0.0 copy-done.1
  42.7 0.7 %copy.15 = bf16[1024,128]{1,0:T(8,128)(2,1)} copy(bf16[1024,128]{1,0:T(8,128)(2,1)S(1)} %copy-done.1) | data formatting | bytes 524288
  43.4 0.0 copy-done
  43.4 0.8 %copy.16 = f32[1024,128]{1,0:T(8,128)} copy(f32[1024,128]{1,0:T(8,128)S(1)} %copy-done) | data formatting | bytes 1048576
Async XLA Ops:
  40.9 1.8 %copy-start.1 = (bf16[1024,128]{1,0:T(8,128)(2,1)S(1)}, bf16[1024,128]{1,0:T(8,128)(2,1)}, u32[]{:S(2)}) copy-start(bf16[1024,128]{1,0:T(8,128)(2,1)} %get-tuple-element.7) | copy-start | bytes 786436
  40.9 2.5 %copy-start = (f32[1024,128]{1,0:T(8,128)S(1)}, f32[1024,128]{1,0:T(8,128)}, u32[]{:S(2)}) copy-start(f32[1024,128]{1,0:T(8,128)} %get-tuple-element.8) | copy-start | bytes 1572868

commit v4 on v3

v4 whole, which is shorter than its diff:
```python
from functools import partial

import jax
import jax.numpy as jnp
from jax import lax
from jax.experimental import pallas as pl
from jax.experimental.pallas import tpu as pltpu
from jax.sharding import PartitionSpec as P

f32 = jnp.float32
bf16 = jnp.bfloat16
MESH = pl.DeviceIdType.MESH
N = 16
LANES = 128
TOK = 1024
EXT = TOK + 16
OWN = 8
CHUNKS = 4
ROWS = 64
HOME = 48
EDGE = 16


PARTNERS = sorted(
    ((x, z, c) for x in range(2) for z in range(4) for c in range(2) if x + z + c),
    key=lambda k: -2 * k[0] - min(k[1], 4 - k[1]),
)


def partner(me, k):
    x = lax.rem(me // 8 + k[0], 2)
    z = lax.rem(lax.rem(me // 2, 4) + k[1], 4)
    return 8 * x + 2 * z + lax.rem(lax.rem(me, 2) + k[2], 2)


def kernel(
    pf_in, ps_in, og_in, up_in, fr_in, c1_in, c2_in, sk_in,
    out_first, out_second, out_filter,
    v_first, v_second, v_filter,
    pf, ps, og, up, fr, c1, c2, sk,
    halo, sbuf, rbuf, ybuf, rret, tok, pick,
    pfx, psx, fc, sc, gg, fg, sg,
    gin, fin, frp, ls, acc, y,
    halo_send, halo_recv, send_sem, recv_sem, local_sem, in_sem, out_sem,
):
    me = lax.axis_index("seq")
    nxt = lax.rem(me + 1, N)
    prv = lax.rem(me + N - 1, N)

    barrier = pltpu.get_barrier_semaphore()

    def greet(k, _):
        pl.semaphore_signal(
            barrier, inc=1, device_id={"seq": lax.rem(me + k, N)}, device_id_type=MESH
        )
        return 0

    lax.fori_loop(1, N, greet, 0)

    fetched = [
        pltpu.make_async_copy(src, dst, in_sem.at[n])
        for n, (src, dst) in enumerate(
            (
                (og_in, og),
                (up_in, up),
                (fr_in, fr),
                (pf_in, pf),
                (ps_in, ps),
                (c1_in, c1),
                (c2_in, c2),
                (sk_in, sk),
            )
        )
    ]
    for copy in fetched:
        copy.start()

    row2 = lax.broadcasted_iota(jnp.int32, (512, 512), 0)
    col2 = lax.broadcasted_iota(jnp.int32, (512, 512), 1)
    picked = ((row2 & 6) << 6) + (row2 & 120) + ((row2 >> 7) << 1) + (row2 & 1)
    pick[...] = (picked == col2).astype(f32).astype(bf16)
    row1 = lax.broadcasted_iota(jnp.int32, (256, 256), 0)
    col1 = lax.broadcasted_iota(jnp.int32, (256, 256), 1)
    source = ((row1 & 64) << 1) + ((row1 >> 7) << 6) + 63 - (row1 & 63)
    flip = (source == col1).astype(f32).astype(bf16)

    def put(base, pairs):
        wide = [jnp.concatenate(pairs[n : n + 2], axis=1) for n in (0, 2)]
        turned = lax.dot_general(
            pick[...],
            jnp.concatenate(wide, axis=0),
            (((1,), (1,)), ((), ())),
            preferred_element_type=f32,
        )
        both = jnp.concatenate(
            [
                turned[:, LANES * n : LANES * (n + 1)].reshape(CHUNKS, N, OWN, LANES)
                for n in range(2)
            ],
            axis=2,
        ).astype(bf16)
        for chunk in range(CHUNKS):
            sbuf[chunk, :, base : base + 16, :] = both[chunk]

    def backwards(quarters):
        wide = jnp.concatenate(quarters[::-1], axis=1)
        back = jnp.dot(flip, wide, preferred_element_type=f32).astype(bf16)
        return [
            jnp.concatenate(
                [
                    back[LANES * z : LANES * (z + 1), LANES * q : LANES * (q + 1)]
                    for z in range(2)
                ],
                axis=1,
            )
            for q in range(len(quarters))
        ]

    def paired(blocks):
        return [jnp.concatenate(blocks[n : n + 2], axis=1) for n in range(0, len(blocks), 2)]

    def blocks_of(ref, size):
        return [ref[size * i : size * (i + 1), :] for i in range(TOK // size)]

    partners = [partner(me, k) for k in PARTNERS]

    def exchange(chunk):
        for to in partners:
            pltpu.make_async_remote_copy(
                src_ref=sbuf.at[chunk, to],
                dst_ref=rbuf.at[chunk, me],
                send_sem=send_sem.at[chunk, to],
                recv_sem=recv_sem.at[chunk, me],
                device_id={"seq": to},
                device_id_type=MESH,
            ).start()
        pltpu.make_async_copy(
            sbuf.at[chunk, me], rbuf.at[chunk, me], local_sem.at[chunk]
        ).start()

    def arrived(chunk):
        def go(k, _):
            frm = lax.rem(me + k, N)
            pltpu.make_async_remote_copy(
                src_ref=sbuf.at[chunk, frm],
                dst_ref=rbuf.at[chunk, frm],
                send_sem=send_sem.at[chunk, frm],
                recv_sem=recv_sem.at[chunk, frm],
                device_id={"seq": frm},
                device_id_type=MESH,
            ).wait()
            return 0

        pltpu.make_async_copy(
            sbuf.at[chunk, me], rbuf.at[chunk, me], local_sem.at[chunk]
        ).wait()
        lax.fori_loop(1, N, go, 0)

    fetched[0].wait()
    fetched[1].wait()
    gg[0:TOK, :] = (og[...].astype(f32) * up[...].astype(f32)).astype(bf16)
    put(0, paired(blocks_of(gg, LANES)))
    fetched[2].wait()
    put(16, backwards(blocks_of(fr, 256)))

    for copy in fetched[3:]:
        copy.wait()

    def convolve(start, size):
        for x, w, dst in ((pfx, c1, fc), (psx, c2, sc)):
            dst[start : start + size, :] = (
                w[0:1, :] * x[EDGE + start : EDGE + start + size, :]
                + w[1:2, :] * x[EDGE + start - 1 : EDGE + start - 1 + size, :]
                + w[2:3, :] * x[EDGE + start - 2 : EDGE + start - 2 + size, :]
            )

    def products(quarters):
        return [
            (fc[256 * q : 256 * (q + 1), :] * sc[256 * q : 256 * (q + 1), :]).astype(bf16)
            for q in quarters
        ]

    for x, src in ((pfx, pf), (psx, ps)):
        x[EDGE : EDGE + TOK, :] = src[...].astype(f32)
    for x in (pfx, psx):
        x[0:EDGE, :] = jnp.zeros((EDGE, LANES), f32)
    convolve(0, TOK)
    put(32, backwards(products(range(4))))
    row3 = lax.broadcasted_iota(jnp.int32, (LANES, 2 * EDGE), 0)
    col3 = lax.broadcasted_iota(jnp.int32, (LANES, 2 * EDGE), 1)
    head = (row3 + col3 == 63) & (col3 < 2)
    tail = (row3 - col3 == 127 - 31) & (col3 >= 30)
    edge_pick = (head | tail).astype(f32).astype(bf16)
    edges = jnp.concatenate(
        [
            jnp.dot(
                edge_pick,
                jnp.concatenate([x[0:EDGE, :], x[TOK - EDGE : TOK, :]], axis=0),
                preferred_element_type=f32,
            ).astype(bf16)
            for x in (pf, ps)
        ],
        axis=1,
    )
    put(48, [edges] * 4)

    pl.semaphore_wait(barrier, N - 1)

    halos = [
        (pf_in, TOK - EDGE, nxt),
        (ps_in, TOK - EDGE, nxt),
        (pf_in, 0, prv),
        (ps_in, 0, prv),
        (og_in, 0, prv),
        (up_in, 0, prv),
    ]
    halo_copies = [
        pltpu.make_async_remote_copy(
            src_ref=ref.at[pl.ds(start, EDGE), :],
            dst_ref=halo.at[n],
            send_sem=halo_send.at[n],
            recv_sem=halo_recv.at[n],
            device_id={"seq": to},
            device_id_type=MESH,
        )
        for n, (ref, start, to) in enumerate(halos)
    ]
    for copy in halo_copies:
        copy.start()

    exchange(0)
    exchange(1)

    frp[...] = jnp.zeros_like(frp)
    gin[32] = jnp.zeros((OWN, LANES), f32)
    y[64:] = jnp.zeros((2, OWN, LANES), f32)

    def unpack_gated(chunk):
        rows = rbuf[chunk, :, 0:16, :].astype(f32)
        gin[0:32, :, :] = rows.reshape(32, OWN, LANES)

    lane = lax.broadcasted_iota(jnp.int32, (OWN, LANES), 1)
    place = lax.broadcasted_iota(jnp.int32, (OWN, LANES), 0)

    def taps(chunk):
        mine = OWN * me + 2 * chunk + (place & 1)
        for k in range(3):
            both = jnp.where((place & 2) == 0, c1[k : k + 1, :], c2[k : k + 1, :])
            yield jnp.sum(jnp.where(lane == mine, both, 0.0), axis=1, keepdims=True)

    def unpack_edges(chunk):
        w = list(taps(chunk))
        at63 = lane == 63
        fill = ((place & 6) == 4) & (at63 | (lane == 62))
        last = jnp.zeros((OWN, LANES), f32)
        for s in range(N):
            own = rbuf[chunk, s, 48:64, :].astype(f32)[0:OWN]
            one = jnp.where(at63, last, pltpu.roll(own, LANES - 1, 1))
            two = jnp.where(at63, pltpu.roll(last, 1, 1), pltpu.roll(last, LANES - 1, 1))
            conv = w[0] * own + w[1] * one + w[2] * two
            product = (conv * pltpu.roll(conv, 6, 0)).astype(bf16).astype(f32)
            i = 2 * (N - 1 - s) + 1
            fin[1, i] = jnp.where(fill, product, fin[1, i])
            last = pltpu.roll(own, 64, 1)

    def unpack_filter(chunk, f):
        for s in range(N):
            rows = rbuf[chunk, N - 1 - s, 16 * f + 16 : 16 * f + 32, :].astype(f32)
            fin[f, 2 * s : 2 * s + 2, :, :] = rows.reshape(2, OWN, LANES)

    row = lax.broadcasted_iota(jnp.int32, (64, LANES), 0)
    col = lax.broadcasted_iota(jnp.int32, (64, LANES), 1)
    mask = col - row <= 64
    low = col < 64

    def rolled(jj, ch):
        line = gin[jj // 4, pl.ds(2 * (jj % 4) + ch, 1), :]
        return pltpu.roll(
            jnp.broadcast_to(line, (64, LANES)), 65, 1, stride=1, stride_axis=0
        )

    def channel(ch, _):
        for z in range(2):
            for f in range(2):
                for u in range(2):
                    frp[z, f, pl.ds(u, 32, stride=2), :] = fin[f, :, 4 * u + 2 * z + ch, :]
        for r in range(16):
            for z in range(2):
                for f in range(2):
                    ls[r, z, f] = frp[z, f, pl.ds(r, 112), :].astype(bf16)
        acc[...] = jnp.zeros_like(acc)
        lines = [rolled(0, ch)]
        hankel = []

        def more_blocks(count):
            while len(hankel) < count:
                lines.append(rolled(min(len(lines), 128), ch))
                hankel.append(jnp.where(mask, lines[-2], lines[-1]).astype(bf16))

        for group in range(4):
            rows = 16 * (group + 1)
            top = 16 * (3 - group)
            left, right = [], []
            for k in range(16):
                j = 16 * group + k
                left.append(ls[15 - k, :, :, top : top + rows, :].reshape(4 * rows, LANES))
                more_blocks(2 * j + 4)
                for n in (2 * j, 2 * j + 1):
                    right.append(jnp.concatenate(hankel[n : n + 3], axis=1))
            left = jnp.concatenate(left, axis=1)
            right = jnp.concatenate(right, axis=0)
            both = jnp.dot(left, right[:, 0:256], preferred_element_type=f32)
            more = jnp.dot(left[2 * rows :], right[:, 256:], preferred_element_type=f32)
            acc[:, :, 0:rows, 0:256] += both.reshape(2, 2, rows, 256)
            acc[1, :, 0:rows, 256:] += more.reshape(2, rows, LANES)
        for f in range(2):
            moved = [
                pltpu.roll(acc[1, f, :, LANES * n : LANES * (n + 1)], 64, 1)
                for n in range(3)
            ]
            for h in range(2):
                total = acc[0, f, :, LANES * h : LANES * (h + 1)] + jnp.where(
                    low, moved[h], moved[h + 1]
                )
                y[0:64, 4 * h + 2 * f + ch, :] = total * (1.0, (TOK * N) ** -0.5)[f]
        return 0

    def home(chunk, to, frm):
        rows = pl.ds(pl.multiple_of(32 * to, 32), HOME)
        return ybuf.at[chunk, rows, :], rret.at[chunk, frm]

    def back(chunk):
        ybuf[chunk] = y[...].reshape(66 * OWN, LANES).astype(bf16)
        for to in partners:
            src, dst = home(chunk, to, me)
            pltpu.make_async_remote_copy(
                src_ref=src,
                dst_ref=dst,
                send_sem=send_sem.at[CHUNKS + chunk, to],
                recv_sem=recv_sem.at[CHUNKS + chunk, me],
                device_id={"seq": to},
                device_id_type=MESH,
            ).start()
        src, dst = home(chunk, me, me)
        pltpu.make_async_copy(src, dst, local_sem.at[CHUNKS + chunk]).start()

    def back_done(chunk):
        def go(k, _):
            frm = lax.rem(me + k, N)
            src, dst = home(chunk, frm, frm)
            pltpu.make_async_remote_copy(
                src_ref=src,
                dst_ref=dst,
                send_sem=send_sem.at[CHUNKS + chunk, frm],
                recv_sem=recv_sem.at[CHUNKS + chunk, frm],
                device_id={"seq": frm},
                device_id_type=MESH,
            ).wait()
            return 0

        src, dst = home(chunk, me, me)
        pltpu.make_async_copy(src, dst, local_sem.at[CHUNKS + chunk]).wait()
        lax.fori_loop(1, N, go, 0)

    def one_chunk(chunk, _):
        arrived(chunk)

        @pl.when(chunk < CHUNKS - 2)
        def _():
            exchange(chunk + 2)

        unpack_gated(chunk)
        unpack_filter(chunk, 0)
        unpack_filter(chunk, 1)
        unpack_edges(chunk)
        lax.fori_loop(0, 2, channel, 0)
        back(chunk)
        return 0

    lax.fori_loop(0, CHUNKS, one_chunk, 0)

    for copy in halo_copies:
        copy.wait()
    before = me > 0
    after = me < N - 1
    for n, x in enumerate((pfx, psx)):
        x[0:EDGE, :] = jnp.where(before, halo[n].astype(f32), 0.0)
        x[EDGE + TOK :, :] = halo[n + 2].astype(f32)
    convolve(0, EDGE)
    convolve(TOK, EXT - TOK)
    gg[TOK:, :] = jnp.where(after, halo[4].astype(f32) * halo[5].astype(f32), 0.0).astype(bf16)

    def columns(chunk, pair):
        both = rret[chunk, :, 16 * pair : 16 * pair + 16, :].astype(f32)
        both = both.reshape(N, 2, OWN, LANES)
        for n in range(2):
            turned = jnp.transpose(both[:, n].reshape(LANES, LANES))
            tok[chunk, 2 * pair + n] = turned.astype(bf16)

    skip = sk[...]

    def grads(start, size, mix):
        at = pl.ds(start, size)
        total = mix + skip * gg[at, :].astype(f32)
        fg[at, :] = (total * sc[at, :]).astype(bf16).astype(f32)
        sg[at, :] = (total * fc[at, :]).astype(bf16).astype(f32)

    for chunk in range(CHUNKS):
        back_done(chunk)
        for pair in range(3):
            columns(chunk, pair)
    for i in range(5):
        both = jnp.dot(
            jnp.concatenate([tok[chunk, i] for chunk in range(CHUNKS)], axis=1),
            pick[...],
            preferred_element_type=f32,
        )
        if i == 4:
            grads(TOK, EXT - TOK, both[0 : EXT - TOK, 0:LANES])
            break
        for h in range(2):
            at = 256 * i + LANES * h
            grads(at, LANES, both[:, 256 * h : 256 * h + LANES])
            v_filter[at : at + LANES, :] = both[:, 256 * h + LANES : 256 * h + 256]
    copies = [
        pltpu.make_async_copy(src, dst, out_sem.at[n])
        for n, (src, dst) in enumerate(
            ((v_filter, out_filter), (v_first, out_first), (v_second, out_second))
        )
    ]
    copies[0].start()
    for x, w, dst, copy in ((fg, c1, v_first, copies[1]), (sg, c2, v_second, copies[2])):
        dst[...] = (
            w[0:1, :] * x[0:TOK, :]
            + w[1:2, :] * x[1 : TOK + 1, :]
            + w[2:3, :] * x[2 : TOK + 2, :]
        ).astype(bf16)
        copy.start()
    for copy in copies:
        copy.wait()


def body(pf, ps, og, up, fr, c1, c2, sk):
    hbm = pl.BlockSpec(memory_space=pltpu.HBM)
    dma = pltpu.SemaphoreType.DMA
    return pl.pallas_call(
        kernel,
        out_shape=(
            jax.ShapeDtypeStruct((TOK, LANES), bf16),
            jax.ShapeDtypeStruct((TOK, LANES), bf16),
            jax.ShapeDtypeStruct((TOK, LANES), f32),
        ),
        in_specs=[hbm] * 8,
        out_specs=(hbm,) * 3,
        scratch_shapes=[
            *[pltpu.VMEM((TOK, LANES), bf16)] * 2,
            pltpu.VMEM((TOK, LANES), f32),
            *[pltpu.VMEM((TOK, LANES), bf16)] * 5,
            *[pltpu.VMEM((3, LANES), f32)] * 2,
            pltpu.VMEM((1, LANES), f32),
            pltpu.VMEM((6, EDGE, LANES), bf16),
            pltpu.VMEM((CHUNKS, N, ROWS, LANES), bf16),
            pltpu.VMEM((CHUNKS, N, ROWS, LANES), bf16),
            pltpu.VMEM((CHUNKS, 66 * OWN, LANES), bf16),
            pltpu.VMEM((CHUNKS, N, HOME, LANES), bf16),
            pltpu.VMEM((CHUNKS, 6, LANES, LANES), bf16),
            pltpu.VMEM((512, 512), bf16),
            pltpu.VMEM((EDGE + EXT, LANES), f32),
            pltpu.VMEM((EDGE + EXT, LANES), f32),
            pltpu.VMEM((EXT, LANES), f32),
            pltpu.VMEM((EXT, LANES), f32),
            pltpu.VMEM((EXT, LANES), bf16),
            pltpu.VMEM((EXT, LANES), f32),
            pltpu.VMEM((EXT, LANES), f32),
            pltpu.VMEM((33, OWN, LANES), f32),
            pltpu.VMEM((2, 32, OWN, LANES), f32),
            pltpu.VMEM((2, 2, 128, LANES), f32),
            pltpu.VMEM((16, 2, 2, 112, LANES), bf16),
            pltpu.VMEM((2, 2, 64, 3 * LANES), f32),
            pltpu.VMEM((66, OWN, LANES), f32),
            dma((6,)),
            dma((6,)),
            dma((2 * CHUNKS, N)),
            dma((2 * CHUNKS, N)),
            dma((2 * CHUNKS,)),
            dma((8,)),
            dma((3,)),
        ],
        compiler_params=pltpu.CompilerParams(
            collective_id=0, has_side_effects=True, vmem_limit_bytes=56 * 2**20
        ),
        cost_estimate=pl.CostEstimate(
            flops=2 * 4 * 10**9, bytes_accessed=3 * 10**6, transcendentals=0
        ),
    )(pf, ps, og, up, fr, c1, c2, sk.reshape(1, LANES))


def solution(mesh):
    tok = P("seq", "ch")
    return jax.shard_map(
        body,
        mesh=mesh,
        in_specs=(tok,) * 5 + (P(None, "ch"), P(None, "ch"), P("ch")),
        out_specs=(tok,) * 3,
        check_vma=False,
    )
```

time: 44.3 us -> 43 us (0.971)
  Pallas kernels: 40.3 us -> 39 us
    pallas_call x1, Pallas kernels: 40.3 us -> 39 us  [body(): pl.pallas_call(kernel, out_shape=(jax.ShapeDtypeStruct((TOK, LANES), bf16...]
where the time goes in v4:
time: 43 us; the launch traced here: 42.9 us
  Pallas kernels  39 us (91%)
  local copies, waits for them, and re-layouts  3.24 us (8%)
  between operations  0.66 us (2%)
    pallas_call x1, Pallas kernels, body(): pl.pallas_call(kernel, out_shape=(jax.ShapeDtypeStruct((TOK, LANES), bf16...  39 us
    unnamed x7, local copies, waits for them, and re-layouts  3.24 us

profile of v4, /device:TPU:1, one launch (start us, length us, event | category | flops | bytes accessed | tf_op | source)
XLA Modules:
  0.0 42.9 jit_solution(17312596978082379708)
XLA Ops:
  0.6 39.0 %shard_map.103 = (bf16[1024,128]{1,0:T(8,128)(2,1)}, bf16[1024,128]{1,0:T(8,128)(2,1)}, f32[1024,128]{1,0:T(8,128)}) custom-call(bf16[1024,128]{1,0:T(8,128)(2,1)} %pf_in.1, bf16[1024,128]{1,0:T(8,128)(2,1)} %ps_in.1, bf16[1024,128]{1,0:T(8,128)(2,1)} %og_in.1, bf16[1024,128]{1,0:T(8,128)(2,1)} %up_in.1, bf16[1024,128]{1,0:T(8,128)(2,1)} %fr_in.1, ...), custom_call_target="tpu_custom_call" | custom-call | flops 8000000000 | bytes 3000000 | tf_op jit(solution)/shard_map/pallas_call | solution.py:446
  39.6 0.0 copy-start.1
  39.6 0.0 copy-start
  39.6 1.7 %copy.14 = bf16[1024,128]{1,0:T(8,128)(2,1)} copy(bf16[1024,128]{1,0:T(8,128)(2,1)} %get-tuple-element.6) | data formatting | bytes 524288
  41.4 0.0 copy-done.1
  41.4 0.7 %copy.15 = bf16[1024,128]{1,0:T(8,128)(2,1)} copy(bf16[1024,128]{1,0:T(8,128)(2,1)S(1)} %copy-done.1) | data formatting | bytes 524288
  42.1 0.0 copy-done
  42.1 0.8 %copy.16 = f32[1024,128]{1,0:T(8,128)} copy(f32[1024,128]{1,0:T(8,128)S(1)} %copy-done) | data formatting | bytes 1048576
Async XLA Ops:
  39.6 1.8 %copy-start.1 = (bf16[1024,128]{1,0:T(8,128)(2,1)S(1)}, bf16[1024,128]{1,0:T(8,128)(2,1)}, u32[]{:S(2)}) copy-start(bf16[1024,128]{1,0:T(8,128)(2,1)} %get-tuple-element.7) | copy-start | bytes 786436
  39.6 2.5 %copy-start = (f32[1024,128]{1,0:T(8,128)S(1)}, f32[1024,128]{1,0:T(8,128)}, u32[]{:S(2)}) copy-start(f32[1024,128]{1,0:T(8,128)} %get-tuple-element.8) | copy-start | bytes 1572868

commit v5 on v4

--- a/solution.py
+++ b/solution.py
@@ -16,8 +16,8 @@
 EXT = TOK + 16
 OWN = 8
 CHUNKS = 4
-ROWS = 64
-HOME = 48
+ROWS = 48
+HOME = 32
 EDGE = 16
 
 
@@ -38,7 +38,7 @@
     out_first, out_second, out_filter,
     v_first, v_second, v_filter,
     pf, ps, og, up, fr, c1, c2, sk,
-    halo, sbuf, rbuf, ybuf, rret, tok, pick,
+    halo, sbuf, rbuf, ybuf, rret, tok, pick, ylast, first, heads,
     pfx, psx, fc, sc, gg, fg, sg,
     gin, fin, frp, ls, acc, y,
     halo_send, halo_recv, send_sem, recv_sem, local_sem, in_sem, out_sem,
@@ -83,6 +83,7 @@
     col1 = lax.broadcasted_iota(jnp.int32, (256, 256), 1)
     source = ((row1 & 64) << 1) + ((row1 >> 7) << 6) + 63 - (row1 & 63)
     flip = (source == col1).astype(f32).astype(bf16)
+    eye = (row1 == col1)[0:LANES, 0:LANES].astype(f32).astype(bf16)
 
     def put(base, pairs):
         wide = [jnp.concatenate(pairs[n : n + 2], axis=1) for n in (0, 2)]
@@ -124,26 +125,31 @@
 
     partners = [partner(me, k) for k in PARTNERS]
 
+    def sent(chunk, to, frm):
+        part = pl.ds(0, ROWS + 16 if isinstance(chunk, int) and chunk == 0 else ROWS)
+        return sbuf.at[chunk, to, part], rbuf.at[chunk, frm, part]
+
     def exchange(chunk):
         for to in partners:
+            src, dst = sent(chunk, to, me)
             pltpu.make_async_remote_copy(
-                src_ref=sbuf.at[chunk, to],
-                dst_ref=rbuf.at[chunk, me],
+                src_ref=src,
+                dst_ref=dst,
                 send_sem=send_sem.at[chunk, to],
                 recv_sem=recv_sem.at[chunk, me],
                 device_id={"seq": to},
                 device_id_type=MESH,
             ).start()
-        pltpu.make_async_copy(
-            sbuf.at[chunk, me], rbuf.at[chunk, me], local_sem.at[chunk]
-        ).start()
+        src, dst = sent(chunk, me, me)
+        pltpu.make_async_copy(src, dst, local_sem.at[chunk]).start()
 
     def arrived(chunk):
         def go(k, _):
             frm = lax.rem(me + k, N)
+            src, dst = sent(chunk, frm, frm)
             pltpu.make_async_remote_copy(
-                src_ref=sbuf.at[chunk, frm],
-                dst_ref=rbuf.at[chunk, frm],
+                src_ref=src,
+                dst_ref=dst,
                 send_sem=send_sem.at[chunk, frm],
                 recv_sem=recv_sem.at[chunk, frm],
                 device_id={"seq": frm},
@@ -151,9 +157,8 @@
             ).wait()
             return 0
 
-        pltpu.make_async_copy(
-            sbuf.at[chunk, me], rbuf.at[chunk, me], local_sem.at[chunk]
-        ).wait()
+        src, dst = sent(chunk, me, me)
+        pltpu.make_async_copy(src, dst, local_sem.at[chunk]).wait()
         lax.fori_loop(1, N, go, 0)
 
     fetched[0].wait()
@@ -200,9 +205,18 @@
             ).astype(bf16)
             for x in (pf, ps)
         ],
-        axis=1,
+        axis=0,
     )
-    put(48, [edges] * 4)
+    turned = [
+        lax.dot_general(
+            eye,
+            edges[LANES * z : LANES * (z + 1)],
+            (((1,), (1,)), ((), ())),
+            preferred_element_type=f32,
+        ).reshape(N, OWN, LANES)
+        for z in range(2)
+    ]
+    sbuf[0, :, ROWS : ROWS + 16, :] = jnp.concatenate(turned, axis=1).astype(bf16)
 
     pl.semaphore_wait(barrier, N - 1)
 
@@ -228,12 +242,12 @@
     for copy in halo_copies:
         copy.start()
 
-    exchange(0)
-    exchange(1)
+    for chunk in range(CHUNKS):
+        exchange(chunk)
 
     frp[...] = jnp.zeros_like(frp)
     gin[32] = jnp.zeros((OWN, LANES), f32)
-    y[64:] = jnp.zeros((2, OWN, LANES), f32)
+    y[64] = jnp.zeros((OWN, LANES), f32)
 
     def unpack_gated(chunk):
         rows = rbuf[chunk, :, 0:16, :].astype(f32)
@@ -242,26 +256,28 @@
     lane = lax.broadcasted_iota(jnp.int32, (OWN, LANES), 1)
     place = lax.broadcasted_iota(jnp.int32, (OWN, LANES), 0)
 
-    def taps(chunk):
-        mine = OWN * me + 2 * chunk + (place & 1)
+    def taps(ref):
+        mine = lane == OWN * me + place
         for k in range(3):
-            both = jnp.where((place & 2) == 0, c1[k : k + 1, :], c2[k : k + 1, :])
-            yield jnp.sum(jnp.where(lane == mine, both, 0.0), axis=1, keepdims=True)
-
-    def unpack_edges(chunk):
-        w = list(taps(chunk))
+            yield jnp.sum(jnp.where(mine, ref[k : k + 1, :], 0.0), axis=1, keepdims=True)
+
+    def unpack_edges():
+        weights = [list(taps(ref)) for ref in (c1, c2)]
         at63 = lane == 63
-        fill = ((place & 6) == 4) & (at63 | (lane == 62))
-        last = jnp.zeros((OWN, LANES), f32)
+        last = [jnp.zeros((OWN, LANES), f32)] * 2
         for s in range(N):
-            own = rbuf[chunk, s, 48:64, :].astype(f32)[0:OWN]
-            one = jnp.where(at63, last, pltpu.roll(own, LANES - 1, 1))
-            two = jnp.where(at63, pltpu.roll(last, 1, 1), pltpu.roll(last, LANES - 1, 1))
-            conv = w[0] * own + w[1] * one + w[2] * two
-            product = (conv * pltpu.roll(conv, 6, 0)).astype(bf16).astype(f32)
-            i = 2 * (N - 1 - s) + 1
-            fin[1, i] = jnp.where(fill, product, fin[1, i])
-            last = pltpu.roll(own, 64, 1)
+            rows = rbuf[0, s, ROWS : ROWS + 16, :].astype(f32)
+            conv = []
+            for z in range(2):
+                own = rows[OWN * z : OWN * (z + 1)]
+                w = weights[z]
+                one = jnp.where(at63, last[z], pltpu.roll(own, LANES - 1, 1))
+                two = jnp.where(
+                    at63, pltpu.roll(last[z], 1, 1), pltpu.roll(last[z], LANES - 1, 1)
+                )
+                conv.append(w[0] * own + w[1] * one + w[2] * two)
+                last[z] = pltpu.roll(own, 64, 1)
+            first[N - 1 - s] = (conv[0] * conv[1]).astype(bf16).astype(f32)
 
     def unpack_filter(chunk, f):
         for s in range(N):
@@ -272,6 +288,7 @@
     col = lax.broadcasted_iota(jnp.int32, (64, LANES), 1)
     mask = col - row <= 64
     low = col < 64
+    fill = ((col == 62) | (col == 63))[0:N]
 
     def rolled(jj, ch):
         line = gin[jj // 4, pl.ds(2 * (jj % 4) + ch, 1), :]
@@ -279,11 +296,15 @@
             jnp.broadcast_to(line, (64, LANES)), 65, 1, stride=1, stride_axis=0
         )
 
-    def channel(ch, _):
+    def channel(ch, chunk):
         for z in range(2):
             for f in range(2):
                 for u in range(2):
                     frp[z, f, pl.ds(u, 32, stride=2), :] = fin[f, :, 4 * u + 2 * z + ch, :]
+        at = pl.ds(3, N, stride=4)
+        frp[0, 1, at, :] = jnp.where(
+            fill, first[:, 2 * chunk + ch, :], frp[0, 1, at, :]
+        )
         for r in range(16):
             for z in range(2):
                 for f in range(2):
@@ -323,14 +344,16 @@
                     low, moved[h], moved[h + 1]
                 )
                 y[0:64, 4 * h + 2 * f + ch, :] = total * (1.0, (TOK * N) ** -0.5)[f]
-        return 0
+        heads[:, 2 * chunk + ch, :] = y[pl.ds(4, N, stride=4), ch, :]
+        return chunk
 
     def home(chunk, to, frm):
-        rows = pl.ds(pl.multiple_of(32 * to, 32), HOME)
-        return ybuf.at[chunk, rows, :], rret.at[chunk, frm]
+        if isinstance(chunk, int) and chunk == CHUNKS - 1:
+            return ylast.at[to], rret.at[chunk, frm]
+        rows = pl.ds(pl.multiple_of(HOME * to, HOME), HOME)
+        return ybuf.at[chunk, rows, :], rret.at[chunk, frm, pl.ds(0, HOME)]
 
     def back(chunk):
-        ybuf[chunk] = y[...].reshape(66 * OWN, LANES).astype(bf16)
         for to in partners:
             src, dst = home(chunk, to, me)
             pltpu.make_async_remote_copy(
@@ -363,21 +386,28 @@
         lax.fori_loop(1, N, go, 0)
 
     def one_chunk(chunk, _):
-        arrived(chunk)
-
-        @pl.when(chunk < CHUNKS - 2)
+        @pl.when(chunk > 0)
         def _():
-            exchange(chunk + 2)
+            arrived(chunk)
 
         unpack_gated(chunk)
         unpack_filter(chunk, 0)
         unpack_filter(chunk, 1)
-        unpack_edges(chunk)
-        lax.fori_loop(0, 2, channel, 0)
-        back(chunk)
+        lax.fori_loop(0, 2, channel, chunk)
+
+        @pl.when(chunk < CHUNKS - 1)
+        def _():
+            ybuf[chunk] = y[0:64].reshape(64 * OWN, LANES).astype(bf16)
+            back(chunk)
+
         return 0
 
+    arrived(0)
+    unpack_edges()
     lax.fori_loop(0, CHUNKS, one_chunk, 0)
+    ylast[:, 0:HOME, :] = y[0:64].reshape(N, HOME, LANES).astype(bf16)
+    ylast[:, HOME:, :] = jnp.concatenate([heads[...]] * 2, axis=1).astype(bf16)
+    back(CHUNKS - 1)
 
     for copy in halo_copies:
         copy.wait()
@@ -407,17 +437,16 @@
 
     for chunk in range(CHUNKS):
         back_done(chunk)
-        for pair in range(3):
+        for pair in range(2):
             columns(chunk, pair)
-    for i in range(5):
+    following = rret[CHUNKS - 1, :, HOME:, :].astype(f32)[:, 0:OWN].reshape(LANES, LANES)
+    grads(TOK, EXT - TOK, jnp.transpose(following)[0 : EXT - TOK])
+    for i in range(4):
         both = jnp.dot(
             jnp.concatenate([tok[chunk, i] for chunk in range(CHUNKS)], axis=1),
             pick[...],
             preferred_element_type=f32,
         )
-        if i == 4:
-            grads(TOK, EXT - TOK, both[0 : EXT - TOK, 0:LANES])
-            break
         for h in range(2):
             at = 256 * i + LANES * h
             grads(at, LANES, both[:, 256 * h : 256 * h + LANES])
@@ -459,12 +488,15 @@
             *[pltpu.VMEM((3, LANES), f32)] * 2,
             pltpu.VMEM((1, LANES), f32),
             pltpu.VMEM((6, EDGE, LANES), bf16),
-            pltpu.VMEM((CHUNKS, N, ROWS, LANES), bf16),
-            pltpu.VMEM((CHUNKS, N, ROWS, LANES), bf16),
-            pltpu.VMEM((CHUNKS, 66 * OWN, LANES), bf16),
-            pltpu.VMEM((CHUNKS, N, HOME, LANES), bf16),
-            pltpu.VMEM((CHUNKS, 6, LANES, LANES), bf16),
+            pltpu.VMEM((CHUNKS, N, ROWS + 16, LANES), bf16),
+            pltpu.VMEM((CHUNKS, N, ROWS + 16, LANES), bf16),
+            pltpu.VMEM((CHUNKS - 1, 64 * OWN, LANES), bf16),
+            pltpu.VMEM((CHUNKS, N, HOME + 16, LANES), bf16),
+            pltpu.VMEM((CHUNKS, 4, LANES, LANES), bf16),
             pltpu.VMEM((512, 512), bf16),
+            pltpu.VMEM((N, HOME + 16, LANES), bf16),
+            pltpu.VMEM((N, OWN, LANES), f32),
+            pltpu.VMEM((N, OWN, LANES), f32),
             pltpu.VMEM((EDGE + EXT, LANES), f32),
             pltpu.VMEM((EDGE + EXT, LANES), f32),
             pltpu.VMEM((EXT, LANES), f32),
@@ -477,7 +509,7 @@
             pltpu.VMEM((2, 2, 128, LANES), f32),
             pltpu.VMEM((16, 2, 2, 112, LANES), bf16),
             pltpu.VMEM((2, 2, 64, 3 * LANES), f32),
-            pltpu.VMEM((66, OWN, LANES), f32),
+            pltpu.VMEM((65, OWN, LANES), f32),
             dma((6,)),
             dma((6,)),
             dma((2 * CHUNKS, N)),

time: 43 us -> 42 us (0.977)
  Pallas kernels: 39 us -> 37.9 us
    pallas_call x1, Pallas kernels: 39 us -> 37.9 us  [body(): pl.pallas_call(kernel, out_shape=(jax.ShapeDtypeStruct((TOK, LANES), bf16...]
where the time goes in v5:
time: 42 us; the launch traced here: 41.8 us
  Pallas kernels  37.9 us (90%)
  local copies, waits for them, and re-layouts  3.24 us (8%)
  between operations  0.66 us (2%)
    pallas_call x1, Pallas kernels, body(): pl.pallas_call(kernel, out_shape=(jax.ShapeDtypeStruct((TOK, LANES), bf16...  37.9 us
    unnamed x7, local copies, waits for them, and re-layouts  3.24 us

profile of v5, /device:TPU:1, one launch (start us, length us, event | category | flops | bytes accessed | tf_op | source)
XLA Modules:
  0.0 41.8 jit_solution(2754432642006581830)
XLA Ops:
  0.6 37.9 %shard_map.103 = (bf16[1024,128]{1,0:T(8,128)(2,1)}, bf16[1024,128]{1,0:T(8,128)(2,1)}, f32[1024,128]{1,0:T(8,128)}) custom-call(bf16[1024,128]{1,0:T(8,128)(2,1)} %pf_in.1, bf16[1024,128]{1,0:T(8,128)(2,1)} %ps_in.1, bf16[1024,128]{1,0:T(8,128)(2,1)} %og_in.1, bf16[1024,128]{1,0:T(8,128)(2,1)} %up_in.1, bf16[1024,128]{1,0:T(8,128)(2,1)} %fr_in.1, ...), custom_call_target="tpu_custom_call" | custom-call | flops 8000000000 | bytes 3000000 | tf_op jit(solution)/shard_map/pallas_call | solution.py:475
  38.6 0.0 copy-start.1
  38.6 0.0 copy-start
  38.6 1.7 %copy.14 = bf16[1024,128]{1,0:T(8,128)(2,1)} copy(bf16[1024,128]{1,0:T(8,128)(2,1)} %get-tuple-element.6) | data formatting | bytes 524288
  40.3 0.0 copy-done.1
  40.3 0.7 %copy.15 = bf16[1024,128]{1,0:T(8,128)(2,1)} copy(bf16[1024,128]{1,0:T(8,128)(2,1)S(1)} %copy-done.1) | data formatting | bytes 524288
  41.0 0.0 copy-done
  41.0 0.8 %copy.16 = f32[1024,128]{1,0:T(8,128)} copy(f32[1024,128]{1,0:T(8,128)S(1)} %copy-done) | data formatting | bytes 1048576
Async XLA Ops:
  38.6 1.8 %copy-start.1 = (bf16[1024,128]{1,0:T(8,128)(2,1)S(1)}, bf16[1024,128]{1,0:T(8,128)(2,1)}, u32[]{:S(2)}) copy-start(bf16[1024,128]{1,0:T(8,128)(2,1)} %get-tuple-element.7) | copy-start | bytes 786436
  38.6 2.5 %copy-start = (f32[1024,128]{1,0:T(8,128)S(1)}, f32[1024,128]{1,0:T(8,128)}, u32[]{:S(2)}) copy-start(f32[1024,128]{1,0:T(8,128)} %get-tuple-element.8) | copy-start | bytes 1572868

commit v6 on v5

--- a/solution.py
+++ b/solution.py
@@ -40,7 +40,7 @@
     pf, ps, og, up, fr, c1, c2, sk,
     halo, sbuf, rbuf, ybuf, rret, tok, pick, ylast, first, heads,
     pfx, psx, fc, sc, gg, fg, sg,
-    gin, fin, frp, ls, acc, y,
+    gin, fin, frps, lss, accs, y,
     halo_send, halo_recv, send_sem, recv_sem, local_sem, in_sem, out_sem,
 ):
     me = lax.axis_index("seq")
@@ -245,7 +245,7 @@
     for chunk in range(CHUNKS):
         exchange(chunk)
 
-    frp[...] = jnp.zeros_like(frp)
+    frps[...] = jnp.zeros_like(frps)
     gin[32] = jnp.zeros((OWN, LANES), f32)
     y[64] = jnp.zeros((OWN, LANES), f32)
 
@@ -297,6 +297,7 @@
         )
 
     def channel(ch, chunk):
+        frp, ls, acc = frps.at[ch], lss.at[ch], accs.at[ch]
         for z in range(2):
             for f in range(2):
                 for u in range(2):
@@ -345,7 +346,6 @@
                 )
                 y[0:64, 4 * h + 2 * f + ch, :] = total * (1.0, (TOK * N) ** -0.5)[f]
         heads[:, 2 * chunk + ch, :] = y[pl.ds(4, N, stride=4), ch, :]
-        return chunk
 
     def home(chunk, to, frm):
         if isinstance(chunk, int) and chunk == CHUNKS - 1:
@@ -393,7 +393,8 @@
         unpack_gated(chunk)
         unpack_filter(chunk, 0)
         unpack_filter(chunk, 1)
-        lax.fori_loop(0, 2, channel, chunk)
+        for ch in range(2):
+            channel(ch, chunk)
 
         @pl.when(chunk < CHUNKS - 1)
         def _():
@@ -506,9 +507,9 @@
             pltpu.VMEM((EXT, LANES), f32),
             pltpu.VMEM((33, OWN, LANES), f32),
             pltpu.VMEM((2, 32, OWN, LANES), f32),
-            pltpu.VMEM((2, 2, 128, LANES), f32),
-            pltpu.VMEM((16, 2, 2, 112, LANES), bf16),
-            pltpu.VMEM((2, 2, 64, 3 * LANES), f32),
+            pltpu.VMEM((2, 2, 2, 128, LANES), f32),
+            pltpu.VMEM((2, 16, 2, 2, 112, LANES), bf16),
+            pltpu.VMEM((2, 2, 2, 64, 3 * LANES), f32),
             pltpu.VMEM((65, OWN, LANES), f32),
             dma((6,)),
             dma((6,)),

time: 42 us -> 40.6 us (0.967)
  Pallas kernels: 37.9 us -> 36.6 us
    pallas_call x1, Pallas kernels: 37.9 us -> 36.6 us  [body(): pl.pallas_call(kernel, out_shape=(jax.ShapeDtypeStruct((TOK, LANES), bf16...]
where the time goes in v6:
time: 40.6 us; the launch traced here: 40.5 us
  Pallas kernels  36.6 us (90%)
  local copies, waits for them, and re-layouts  3.24 us (8%)
  between operations  0.66 us (2%)
    pallas_call x1, Pallas kernels, body(): pl.pallas_call(kernel, out_shape=(jax.ShapeDtypeStruct((TOK, LANES), bf16...  36.6 us
    unnamed x7, local copies, waits for them, and re-layouts  3.24 us

profile of v6, /device:TPU:1, one launch (start us, length us, event | category | flops | bytes accessed | tf_op | source)
XLA Modules:
  0.0 40.5 jit_solution(8658696449770409981)
XLA Ops:
  0.6 36.6 %shard_map.103 = (bf16[1024,128]{1,0:T(8,128)(2,1)}, bf16[1024,128]{1,0:T(8,128)(2,1)}, f32[1024,128]{1,0:T(8,128)}) custom-call(bf16[1024,128]{1,0:T(8,128)(2,1)} %pf_in.1, bf16[1024,128]{1,0:T(8,128)(2,1)} %ps_in.1, bf16[1024,128]{1,0:T(8,128)(2,1)} %og_in.1, bf16[1024,128]{1,0:T(8,128)(2,1)} %up_in.1, bf16[1024,128]{1,0:T(8,128)(2,1)} %fr_in.1, ...), custom_call_target="tpu_custom_call" | custom-call | flops 8000000000 | bytes 3000000 | tf_op jit(solution)/shard_map/pallas_call | solution.py:476
  37.2 0.0 copy-start.1
  37.2 0.0 copy-start
  37.2 1.7 %copy.14 = bf16[1024,128]{1,0:T(8,128)(2,1)} copy(bf16[1024,128]{1,0:T(8,128)(2,1)} %get-tuple-element.6) | data formatting | bytes 524288
  39.0 0.0 copy-done.1
  39.0 0.7 %copy.15 = bf16[1024,128]{1,0:T(8,128)(2,1)} copy(bf16[1024,128]{1,0:T(8,128)(2,1)S(1)} %copy-done.1) | data formatting | bytes 524288
  39.7 0.0 copy-done
  39.7 0.8 %copy.16 = f32[1024,128]{1,0:T(8,128)} copy(f32[1024,128]{1,0:T(8,128)S(1)} %copy-done) | data formatting | bytes 1048576
Async XLA Ops:
  37.2 1.8 %copy-start.1 = (bf16[1024,128]{1,0:T(8,128)(2,1)S(1)}, bf16[1024,128]{1,0:T(8,128)(2,1)}, u32[]{:S(2)}) copy-start(bf16[1024,128]{1,0:T(8,128)(2,1)} %get-tuple-element.7) | copy-start | bytes 786436
  37.2 2.5 %copy-start = (f32[1024,128]{1,0:T(8,128)S(1)}, f32[1024,128]{1,0:T(8,128)}, u32[]{:S(2)}) copy-start(f32[1024,128]{1,0:T(8,128)} %get-tuple-element.8) | copy-start | bytes 1572868

commit v7 on v6

--- a/solution.py
+++ b/solution.py
@@ -143,18 +143,27 @@
         src, dst = sent(chunk, me, me)
         pltpu.make_async_copy(src, dst, local_sem.at[chunk]).start()
 
+    def expected(chunk, frm):
+        src, dst = sent(chunk, frm, frm)
+        return pltpu.make_async_remote_copy(
+            src_ref=src,
+            dst_ref=dst,
+            send_sem=send_sem.at[chunk, frm],
+            recv_sem=recv_sem.at[chunk, frm],
+            device_id={"seq": frm},
+            device_id_type=MESH,
+        )
+
+    def all_sent(copy, chunk):
+        def go(k, _):
+            copy(chunk, lax.rem(me + k, N)).wait_send()
+            return 0
+
+        lax.fori_loop(1, N, go, 0)
+
     def arrived(chunk):
         def go(k, _):
-            frm = lax.rem(me + k, N)
-            src, dst = sent(chunk, frm, frm)
-            pltpu.make_async_remote_copy(
-                src_ref=src,
-                dst_ref=dst,
-                send_sem=send_sem.at[chunk, frm],
-                recv_sem=recv_sem.at[chunk, frm],
-                device_id={"seq": frm},
-                device_id_type=MESH,
-            ).wait()
+            expected(chunk, lax.rem(me + k, N)).wait_recv()
             return 0
 
         src, dst = sent(chunk, me, me)
@@ -367,18 +376,20 @@
         src, dst = home(chunk, me, me)
         pltpu.make_async_copy(src, dst, local_sem.at[CHUNKS + chunk]).start()
 
+    def returned(chunk, frm):
+        src, dst = home(chunk, frm, frm)
+        return pltpu.make_async_remote_copy(
+            src_ref=src,
+            dst_ref=dst,
+            send_sem=send_sem.at[CHUNKS + chunk, frm],
+            recv_sem=recv_sem.at[CHUNKS + chunk, frm],
+            device_id={"seq": frm},
+            device_id_type=MESH,
+        )
+
     def back_done(chunk):
         def go(k, _):
-            frm = lax.rem(me + k, N)
-            src, dst = home(chunk, frm, frm)
-            pltpu.make_async_remote_copy(
-                src_ref=src,
-                dst_ref=dst,
-                send_sem=send_sem.at[CHUNKS + chunk, frm],
-                recv_sem=recv_sem.at[CHUNKS + chunk, frm],
-                device_id={"seq": frm},
-                device_id_type=MESH,
-            ).wait()
+            returned(chunk, lax.rem(me + k, N)).wait_recv()
             return 0
 
         src, dst = home(chunk, me, me)
@@ -409,6 +420,8 @@
     ylast[:, 0:HOME, :] = y[0:64].reshape(N, HOME, LANES).astype(bf16)
     ylast[:, HOME:, :] = jnp.concatenate([heads[...]] * 2, axis=1).astype(bf16)
     back(CHUNKS - 1)
+    for chunk in range(CHUNKS):
+        all_sent(expected, chunk)
 
     for copy in halo_copies:
         copy.wait()
@@ -466,6 +479,8 @@
             + w[2:3, :] * x[2 : TOK + 2, :]
         ).astype(bf16)
         copy.start()
+    for chunk in range(CHUNKS):
+        all_sent(returned, chunk)
     for copy in copies:
         copy.wait()
 

time: 40.6 us -> 40.5 us (level)
  no operation moved by 1% of the time
where the time goes in v7:
time: 40.5 us; the launch traced here: 40.4 us
  Pallas kernels  36.5 us (90%)
  local copies, waits for them, and re-layouts  3.24 us (8%)
  between operations  0.66 us (2%)
    pallas_call x1, Pallas kernels, body(): pl.pallas_call(kernel, out_shape=(jax.ShapeDtypeStruct((TOK, LANES), bf16...  36.5 us
    unnamed x7, local copies, waits for them, and re-layouts  3.24 us

profile of v7, /device:TPU:1, one launch (start us, length us, event | category | flops | bytes accessed | tf_op | source)
XLA Modules:
  0.0 40.4 jit_solution(8047633626794229855)
XLA Ops:
  0.6 36.5 %shard_map.103 = (bf16[1024,128]{1,0:T(8,128)(2,1)}, bf16[1024,128]{1,0:T(8,128)(2,1)}, f32[1024,128]{1,0:T(8,128)}) custom-call(bf16[1024,128]{1,0:T(8,128)(2,1)} %pf_in.1, bf16[1024,128]{1,0:T(8,128)(2,1)} %ps_in.1, bf16[1024,128]{1,0:T(8,128)(2,1)} %og_in.1, bf16[1024,128]{1,0:T(8,128)(2,1)} %up_in.1, bf16[1024,128]{1,0:T(8,128)(2,1)} %fr_in.1, ...), custom_call_target="tpu_custom_call" | custom-call | flops 8000000000 | bytes 3000000 | tf_op jit(solution)/shard_map/pallas_call | solution.py:491
  37.1 0.0 copy-start.1
  37.1 0.0 copy-start
  37.1 1.7 %copy.14 = bf16[1024,128]{1,0:T(8,128)(2,1)} copy(bf16[1024,128]{1,0:T(8,128)(2,1)} %get-tuple-element.6) | data formatting | bytes 524288
  38.9 0.0 copy-done.1
  38.9 0.7 %copy.15 = bf16[1024,128]{1,0:T(8,128)(2,1)} copy(bf16[1024,128]{1,0:T(8,128)(2,1)S(1)} %copy-done.1) | data formatting | bytes 524288
  39.6 0.0 copy-done
  39.6 0.8 %copy.16 = f32[1024,128]{1,0:T(8,128)} copy(f32[1024,128]{1,0:T(8,128)S(1)} %copy-done) | data formatting | bytes 1048576
Async XLA Ops:
  37.1 1.8 %copy-start.1 = (bf16[1024,128]{1,0:T(8,128)(2,1)S(1)}, bf16[1024,128]{1,0:T(8,128)(2,1)}, u32[]{:S(2)}) copy-start(bf16[1024,128]{1,0:T(8,128)(2,1)} %get-tuple-element.7) | copy-start | bytes 786436
  37.1 2.5 %copy-start = (f32[1024,128]{1,0:T(8,128)S(1)}, f32[1024,128]{1,0:T(8,128)}, u32[]{:S(2)}) copy-start(f32[1024,128]{1,0:T(8,128)} %get-tuple-element.8) | copy-start | bytes 1572868

commit v8 on v7

--- a/solution.py
+++ b/solution.py
@@ -525,7 +525,7 @@
             pltpu.VMEM((2, 2, 2, 128, LANES), f32),
             pltpu.VMEM((2, 16, 2, 2, 112, LANES), bf16),
             pltpu.VMEM((2, 2, 2, 64, 3 * LANES), f32),
-            pltpu.VMEM((65, OWN, LANES), f32),
+            pltpu.VMEM((72, OWN, LANES), f32),
             dma((6,)),
             dma((6,)),
             dma((2 * CHUNKS, N)),

time: 40.5 us -> 40.5 us (level)
  no operation moved by 1% of the time
where the time goes in v8:
time: 40.5 us; the launch traced here: 40.4 us
  Pallas kernels  36.5 us (90%)
  local copies, waits for them, and re-layouts  3.24 us (8%)
  between operations  0.66 us (2%)
    pallas_call x1, Pallas kernels, body(): pl.pallas_call(kernel, out_shape=(jax.ShapeDtypeStruct((TOK, LANES), bf16...  36.5 us
    unnamed x7, local copies, waits for them, and re-layouts  3.24 us

profile of v8, /device:TPU:1, one launch (start us, length us, event | category | flops | bytes accessed | tf_op | source)
XLA Modules:
  0.0 40.4 jit_solution(6858385252640923533)
XLA Ops:
  0.6 36.5 %shard_map.103 = (bf16[1024,128]{1,0:T(8,128)(2,1)}, bf16[1024,128]{1,0:T(8,128)(2,1)}, f32[1024,128]{1,0:T(8,128)}) custom-call(bf16[1024,128]{1,0:T(8,128)(2,1)} %pf_in.1, bf16[1024,128]{1,0:T(8,128)(2,1)} %ps_in.1, bf16[1024,128]{1,0:T(8,128)(2,1)} %og_in.1, bf16[1024,128]{1,0:T(8,128)(2,1)} %up_in.1, bf16[1024,128]{1,0:T(8,128)(2,1)} %fr_in.1, ...), custom_call_target="tpu_custom_call" | custom-call | flops 8000000000 | bytes 3000000 | tf_op jit(solution)/shard_map/pallas_call | solution.py:491
  37.1 0.0 copy-start.1
  37.1 0.0 copy-start
  37.1 1.7 %copy.14 = bf16[1024,128]{1,0:T(8,128)(2,1)} copy(bf16[1024,128]{1,0:T(8,128)(2,1)} %get-tuple-element.6) | data formatting | bytes 524288
  38.9 0.0 copy-done.1
  38.9 0.7 %copy.15 = bf16[1024,128]{1,0:T(8,128)(2,1)} copy(bf16[1024,128]{1,0:T(8,128)(2,1)S(1)} %copy-done.1) | data formatting | bytes 524288
  39.6 0.0 copy-done
  39.6 0.8 %copy.16 = f32[1024,128]{1,0:T(8,128)} copy(f32[1024,128]{1,0:T(8,128)S(1)} %copy-done) | data formatting | bytes 1048576
Async XLA Ops:
  37.1 1.8 %copy-start.1 = (bf16[1024,128]{1,0:T(8,128)(2,1)S(1)}, bf16[1024,128]{1,0:T(8,128)(2,1)}, u32[]{:S(2)}) copy-start(bf16[1024,128]{1,0:T(8,128)(2,1)} %get-tuple-element.7) | copy-start | bytes 786436
  37.1 2.5 %copy-start = (f32[1024,128]{1,0:T(8,128)S(1)}, f32[1024,128]{1,0:T(8,128)}, u32[]{:S(2)}) copy-start(f32[1024,128]{1,0:T(8,128)} %get-tuple-element.8) | copy-start | bytes 1572868

commit v9 on v8

--- a/solution.py
+++ b/solution.py
@@ -248,11 +248,11 @@
         )
         for n, (ref, start, to) in enumerate(halos)
     ]
+
+    for chunk in range(CHUNKS):
+        exchange(chunk)
     for copy in halo_copies:
         copy.start()
-
-    for chunk in range(CHUNKS):
-        exchange(chunk)
 
     frps[...] = jnp.zeros_like(frps)
     gin[32] = jnp.zeros((OWN, LANES), f32)

time: 40.5 us -> 40.1 us (level)
  Pallas kernels: 36.5 us -> 36 us
    pallas_call x1, Pallas kernels: 36.5 us -> 36 us  [body(): pl.pallas_call(kernel, out_shape=(jax.ShapeDtypeStruct((TOK, LANES), bf16...]
where the time goes in v9:
time: 40.1 us; the launch traced here: 39.9 us
  Pallas kernels  36 us (90%)
  local copies, waits for them, and re-layouts  3.24 us (8%)
  between operations  0.66 us (2%)
    pallas_call x1, Pallas kernels, body(): pl.pallas_call(kernel, out_shape=(jax.ShapeDtypeStruct((TOK, LANES), bf16...  36 us
    unnamed x7, local copies, waits for them, and re-layouts  3.24 us

profile of v9, /device:TPU:1, one launch (start us, length us, event | category | flops | bytes accessed | tf_op | source)
XLA Modules:
  0.0 39.9 jit_solution(8678299775711687145)
XLA Ops:
  0.6 36.0 %shard_map.103 = (bf16[1024,128]{1,0:T(8,128)(2,1)}, bf16[1024,128]{1,0:T(8,128)(2,1)}, f32[1024,128]{1,0:T(8,128)}) custom-call(bf16[1024,128]{1,0:T(8,128)(2,1)} %pf_in.1, bf16[1024,128]{1,0:T(8,128)(2,1)} %ps_in.1, bf16[1024,128]{1,0:T(8,128)(2,1)} %og_in.1, bf16[1024,128]{1,0:T(8,128)(2,1)} %up_in.1, bf16[1024,128]{1,0:T(8,128)(2,1)} %fr_in.1, ...), custom_call_target="tpu_custom_call" | custom-call | flops 8000000000 | bytes 3000000 | tf_op jit(solution)/shard_map/pallas_call | solution.py:491
  36.6 0.0 copy-start.1
  36.7 0.0 copy-start
  36.7 1.7 %copy.14 = bf16[1024,128]{1,0:T(8,128)(2,1)} copy(bf16[1024,128]{1,0:T(8,128)(2,1)} %get-tuple-element.6) | data formatting | bytes 524288
  38.4 0.0 copy-done.1
  38.4 0.7 %copy.15 = bf16[1024,128]{1,0:T(8,128)(2,1)} copy(bf16[1024,128]{1,0:T(8,128)(2,1)S(1)} %copy-done.1) | data formatting | bytes 524288
  39.1 0.0 copy-done
  39.1 0.8 %copy.16 = f32[1024,128]{1,0:T(8,128)} copy(f32[1024,128]{1,0:T(8,128)S(1)} %copy-done) | data formatting | bytes 1048576
Async XLA Ops:
  36.6 1.8 %copy-start.1 = (bf16[1024,128]{1,0:T(8,128)(2,1)S(1)}, bf16[1024,128]{1,0:T(8,128)(2,1)}, u32[]{:S(2)}) copy-start(bf16[1024,128]{1,0:T(8,128)(2,1)} %get-tuple-element.7) | copy-start | bytes 786436
  36.7 2.5 %copy-start = (f32[1024,128]{1,0:T(8,128)S(1)}, f32[1024,128]{1,0:T(8,128)}, u32[]{:S(2)}) copy-start(f32[1024,128]{1,0:T(8,128)} %get-tuple-element.8) | copy-start | bytes 1572868
